TPU v7x, 256 devices: a whole 4x4x8 slice. The times are simulated.
256 devices in a mesh: view: 8 (over z_lo, x), tile: 32 (over y, z_hi, core).
Axes of the slice: x: 4, y: 4, z: 8 (z_hi: 4, z_lo: 2; z = z_hi * 2 + z_lo), core: 2. Of those that a mesh axis runs over, the one named last changes fastest.
Arguments:
- estimate: float32 [16, 1024, 1024], P(None, 'tile', 'view'), may hold values from 0.5 to 2
- measured: bfloat16 [8, 16, 1024, 1024], P('view', None, 'tile'), may hold values from 0.05 to 12
- psf_z: float32 [8, 65], P('view'), may hold values from 0.05 to 1
- psf_xy: float32 [8, 2, 9], P('view'), may hold values from 0.1 to 1
- offsets: int32 [8, 2], P('view'), may hold values from -4 to 4, as said below
- coverage: int32 [8, 32], P('view', 'tile'), may hold values from 0 to 1, as said below
Outputs:
- restored: float32 [16, 1024, 1024], P(None, 'tile', 'view')
Inputs may be any that keep to these rules, and one draw needn't show every extreme that they name: offsets[v, 0] shifts view v along rows and offsets[v, 1] along columns; some view has a row offset of 4 and some view a column offset of -4. coverage[v, t] is 1 where view v images rows t * 32 to (t + 1) * 32 - 1, else 0; every tile is imaged by at least one view.
All inputs are finite; a program needn't handle non-finite values.
Results may differ from a plain program's by a relative error of at most 0.0006.
Values may be sent and summed in bfloat16 or wider, within the bound.
A program may use at most 64 MiB of HBM per device.

v0:
```python
import jax
import jax.numpy as jnp
from jax import lax
from jax.sharding import PartitionSpec as P

SHIFT = 4
ITERS = 2


EXACT_MATMUL = lax.Precision.HIGHEST


def shortened(shard):

    def short(part):
        return part.astype(jnp.bfloat16) if part.dtype == jnp.float32 else part

    return jax.tree.map(short, shard)


def padded(shard, sides, width):
    for axis, dim in sides:
        size, length = (lax.axis_size(axis), shard.shape[dim])
        up = [(i, (i + 1) % size) for i in range(size - 1)]
        down = [(j, i) for i, j in up]
        last = lax.slice_in_dim(shard, length - width, length, axis=dim)
        leading = lax.slice_in_dim(shard, 0, width, axis=dim)
        before = lax.ppermute(last, axis, up)
        after = lax.ppermute(leading, axis, down)
        shard = jnp.concatenate([before, shard, after], axis=dim)
    return shard


def band_stack(kernel, n_in, n_out, lead_offset):
    count_taps = kernel.shape[-1]
    rows_in = jnp.arange(n_in, dtype=jnp.int32)[:, None]
    rows_out = jnp.arange(n_out, dtype=jnp.int32)[None, :]
    tap_ids = jnp.arange(count_taps, dtype=jnp.int32)[:, None, None]
    selector = ((rows_in - rows_out + lead_offset)[None] == tap_ids).astype(jnp.float32)
    return jnp.tensordot(kernel, selector, axes=1, precision=EXACT_MATMUL)


def place_taps(kernel, shifts):
    count_taps = kernel.shape[-1]
    positions = jnp.arange(count_taps + 2 * SHIFT, dtype=jnp.int32)
    tap_ids = jnp.arange(count_taps, dtype=jnp.int32)
    selector = (
        positions[None, None, :] == tap_ids[None, :, None] + SHIFT + shifts[:, None, None]
    ).astype(jnp.float32)
    return jnp.einsum("vt,vtu->vu", kernel, selector, precision=EXACT_MATMUL)


def view_filters(psf_z, psf_xy, offsets, planes, row_count, block_cols):
    z_kernel = psf_z / jnp.sum(psf_z, axis=-1, keepdims=True)
    lateral_kernel = psf_xy / jnp.sum(psf_xy, axis=-1, keepdims=True)
    z_reach = (z_kernel.shape[-1] - 1) // 2
    depth_banded = band_stack(z_kernel, planes, planes, z_reach)
    y_taps = place_taps(lateral_kernel[:, 0], offsets[:, 0])
    x_taps = place_taps(lateral_kernel[:, 1], offsets[:, 1])
    margin = (y_taps.shape[-1] - 1) // 2
    forward = (
        band_stack(y_taps, row_count + 2 * margin, row_count, 0),
        band_stack(x_taps, 2 * block_cols, block_cols, 0),
    )
    backward = (
        band_stack(jnp.flip(y_taps, -1), row_count + 2 * margin, row_count, 0),
        band_stack(jnp.flip(x_taps, -1), 2 * block_cols, block_cols, 0),
    )
    return (depth_banded, forward, backward)


def cross_pass(widened_ratio, x_band, col_total, margin):
    block_cols = x_band.shape[-1]
    lead_shape = widened_ratio.shape[:-1]
    padded_cols = jnp.pad(
        widened_ratio, [(0, 0)] * (widened_ratio.ndim - 1) + [(0, block_cols - 2 * margin)]
    )
    head_blocks = padded_cols[..., :col_total].reshape(
        lead_shape + (col_total // block_cols, block_cols)
    )
    next_blocks = padded_cols[..., block_cols : block_cols + col_total].reshape(
        lead_shape + (col_total // block_cols, block_cols)
    )
    result = jnp.einsum(
        "vzynu,vuc->vzync", head_blocks, x_band[:, :block_cols], precision=EXACT_MATMUL
    )
    result = result + jnp.einsum(
        "vzynu,vuc->vzync", next_blocks, x_band[:, block_cols:], precision=EXACT_MATMUL
    )
    return result.reshape(lead_shape + (col_total,))


def lateral_rows(object_volume, banded_kernels, col_total, margin):
    widened_ratio = padded(shortened(object_volume), (("tile", 2),), margin).astype(
        object_volume.dtype
    )
    object_volume = jnp.einsum(
        "cnkw,ckr->cnrw", widened_ratio, banded_kernels[0], precision=EXACT_MATMUL
    )
    widened_ratio = jnp.pad(object_volume, ((0, 0), (0, 0), (0, 0), (margin, margin)))
    return cross_pass(widened_ratio, banded_kernels[1], col_total, margin)


def body(estimate, measured, psf_z, psf_xy, offsets, coverage):
    planes, row_count, col_count = estimate.shape
    margin = (psf_xy.shape[-1] - 1) // 2 + SHIFT
    current = estimate
    col_total = measured.shape[-1]
    block_cols = 128
    depth_banded, forward, backward = view_filters(
        psf_z, psf_xy, offsets, planes, row_count, block_cols
    )
    covered = coverage[:, 0].astype(jnp.float32)
    view_count = lax.psum(coverage[0, 0], "view").astype(jnp.float32)
    for iteration in range(ITERS):
        blurred = jnp.einsum(
            "rnl,nzf->rlzf",
            depth_banded,
            lax.all_gather(current.astype(jnp.bfloat16), "view", axis=2, tiled=True).astype(
                jnp.float32
            ),
            precision=EXACT_MATMUL,
        )
        blurred = lateral_rows(blurred, forward, col_total, margin)
        measurement_ratios = measured.astype(jnp.float32) / blurred
        updated_estimate = jnp.einsum(
            "rez,rzof->reof", depth_banded, measurement_ratios, precision=EXACT_MATMUL
        )
        updated_estimate = lateral_rows(updated_estimate, backward, col_total, margin)
        log_term = jnp.sum(covered[:, None, None, None] * jnp.log(updated_estimate), axis=0)
        log_total = lax.psum_scatter(log_term, "view", scatter_dimension=2, tiled=True)
        current = current * jnp.exp(log_total / view_count)
    return current


def solution(mesh):
    placed = (
        P(None, "tile", "view"),
        P("view", None, "tile", None),
        P("view", None),
        P("view", None, None),
        P("view", None),
        P("view", "tile"),
    )
    return jax.shard_map(
        body, mesh=mesh, in_specs=placed, out_specs=P(None, "tile", "view"), check_vma=False
    )
```

profile of v0, /device:TPU:48, one launch (start us, length us, event | category | flops | bytes accessed | tf_op | source)
XLA Modules:
  0.0 321.2 jit_solution(6538633816662928004)
XLA Ops:
  6.5 1.8 copy.86
  8.4 1.3 fusion.75
  9.7 1.3 reduce_sum.20
  11.0 0.8 reduce_sum.16
  11.8 0.7 fusion.66
  12.5 0.8 broadcast_divide_fusion
  13.5 0.6 fusion.65
  14.5 1.5 fusion.54
  16.3 35.1 %all-gather.3.cloned.1.call-done = bf16[16,32,1024]{2,0,1:T(8,128)(2,1)} async-done(((bf16[16,32,128]{2,0,1:T(8,128)(2,1)}), bf16[16,32,1024]{2,0,1:T(8,128)(2,1)}) %all-gather.3.cloned.1.call-update) | async-done | bytes 1048592 | tf_op jit(solution)/shard_map/all_gather | solution.py:119
  51.4 2.2 fusion.46
  53.7 1.9 collective-permute-start
  55.6 6.8 %collective-permute-start.1 = (bf16[1,16,8,1024]{3,1,2,0:T(8,128)(2,1)S(1)}, bf16[1,16,8,1024]{3,1,2,0:T(8,128)(2,1)S(1)}, u32[]{:S(2)}, u32[]{:S(2)}) collective-permute-start(bf16[1,16,8,1024]{3,1,2,0:T(8,128)(2,1)S(1)} %get-tuple-element.14), channel_id=1, source_target_pairs={{1,0},{2,1},{3,2},{4,3},{5,4},{6,5},{7,6},{8,7},{9,8},{10,9},{11,1... | collective-permute-start | bytes 786440 | tf_op jit(solution)/shard_map/ppermute | solution.py:29
  62.6 1.2 fusion.2
  63.8 3.3 %collective-permute-done = bf16[1,16,8,1024]{3,1,2,0:T(8,128)(2,1)S(1)} collective-permute-done((bf16[1,16,8,1024]{3,1,2,0:T(8,128)(2,1)S(1)}, bf16[1,16,8,1024]{3,1,2,0:T(8,128)(2,1)S(1)}, u32[]{:S(2)}, u32[]{:S(2)}) %collective-permute-start) | collective-permute-done | bytes 262176 | tf_op jit(solution)/shard_map/ppermute | solution.py:28
  67.3 2.6 convolution_bitcast_fusion.3
  69.9 0.6 pad_slice_fusion.7
  70.5 0.7 pad.26
  72.4 1.9 fusion.18
  74.3 1.8 fusion.26
  76.1 1.9 reshape.288
  78.1 1.9 fusion.4
  80.0 2.8 fusion.51
  82.8 0.8 fusion.73
  83.7 2.0 collective-permute-start.2
  85.7 6.6 %collective-permute-start.3 = (bf16[1,16,8,1024]{3,1,2,0:T(8,128)(2,1)}, bf16[1,16,8,1024]{3,1,2,0:T(8,128)(2,1)}, u32[]{:S(2)}, u32[]{:S(2)}) collective-permute-start(bf16[1,16,8,1024]{3,1,2,0:T(8,128)(2,1)} %get-tuple-element.12), channel_id=1, source_target_pairs={{1,0},{2,1},{3,2},{4,3},{5,4},{6,5},{7,6},{8,7},{9,8},{10,9},{11,1... | collective-permute-start | bytes 786440 | tf_op jit(solution)/shard_map/ppermute | solution.py:29
  93.0 1.2 fusion
  94.2 3.2 collective-permute-done.2
  97.4 1.1 maximum_bitcast_fusion.1
  98.5 2.6 convolution_bitcast_fusion.2
  101.2 0.6 pad_slice_fusion.6
  101.8 0.7 pad.28
  103.7 1.9 fusion.14
  105.6 1.9 log_multiply_fusion.1
  107.4 1.5 mul.37
  108.9 4.1 %copy.12 = f32[16,32,1024]{2,0,1:T(8,128)} copy(f32[16,32,1024]{2,1,0:T(8,128)} %mul.37) | data formatting | bytes 4194304 | tf_op jit(solution)/shard_map/mul | solution.py:130
  113.2 16.1 %psum.7 = s32[]{:T(128)} all-reduce(s32[]{:T(128)} %bitcast.46), channel_id=1, replica_groups=mesh['view'=8,'tile'=32] {'view'}, use_global_device_ids=true, to_apply=%region_3.4 | all-reduce | flops 1 | bytes 8 | tf_op jit(solution)/shard_map/psum | solution.py:114
  129.9 32.0 %reduce-scatter.3.cloned.1.call-done = f32[16,32,128]{2,0,1:T(8,128)} async-done(((f32[16,32,1024]{2,0,1:T(8,128)}), f32[16,32,128]{2,0,1:T(8,128)}) %reduce-scatter.3.cloned.1.call-update) | async-done | bytes 262160 | tf_op jit(solution)/shard_map/reduce_scatter | solution.py:131
  161.9 1.8 fusion.70
  163.9 39.8 %all-gather.5.cloned.1.call-done = bf16[16,32,1024]{2,0,1:T(8,128)(2,1)} async-done(((bf16[16,32,128]{2,0,1:T(8,128)(2,1)}), bf16[16,32,1024]{2,0,1:T(8,128)(2,1)}) %all-gather.5.cloned.1.call-update) | async-done | bytes 1048592 | tf_op jit(solution)/shard_map/all_gather | solution.py:119
  203.8 2.2 fusion.47
  206.1 1.9 collective-permute-start.4
  208.0 6.7 %collective-permute-start.5 = (bf16[1,16,8,1024]{3,1,2,0:T(8,128)(2,1)S(1)}, bf16[1,16,8,1024]{3,1,2,0:T(8,128)(2,1)S(1)}, u32[]{:S(2)}, u32[]{:S(2)}) collective-permute-start(bf16[1,16,8,1024]{3,1,2,0:T(8,128)(2,1)S(1)} %get-tuple-element.10), channel_id=1, source_target_pairs={{1,0},{2,1},{3,2},{4,3},{5,4},{6,5},{7,6},{8,7},{9,8},{10,9},{11,1... | collective-permute-start | bytes 786440 | tf_op jit(solution)/shard_map/ppermute | solution.py:29
  214.7 4.8 %collective-permute-done.4 = bf16[1,16,8,1024]{3,1,2,0:T(8,128)(2,1)S(1)} collective-permute-done((bf16[1,16,8,1024]{3,1,2,0:T(8,128)(2,1)S(1)}, bf16[1,16,8,1024]{3,1,2,0:T(8,128)(2,1)S(1)}, u32[]{:S(2)}, u32[]{:S(2)}) %collective-permute-start.4) | collective-permute-done | bytes 262176 | tf_op jit(solution)/shard_map/ppermute | solution.py:28
  219.7 2.6 convolution_bitcast_fusion.1
  222.4 0.6 pad_slice_fusion.5
  223.0 0.7 pad.30
  224.9 1.9 fusion.10
  226.8 1.8 fusion.31
  228.6 1.5 reshape.298
  230.1 1.9 fusion.5
  232.0 2.8 fusion.48
  234.9 2.0 collective-permute-start.6
  236.9 6.8 %collective-permute-start.7 = (bf16[1,16,8,1024]{3,1,2,0:T(8,128)(2,1)S(1)}, bf16[1,16,8,1024]{3,1,2,0:T(8,128)(2,1)S(1)}, u32[]{:S(2)}, u32[]{:S(2)}) collective-permute-start(bf16[1,16,8,1024]{3,1,2,0:T(8,128)(2,1)S(1)} %get-tuple-element.8), channel_id=1, source_target_pairs={{1,0},{2,1},{3,2},{4,3},{5,4},{6,5},{7,6},{8,7},{9,8},{10,9},{11,1... | collective-permute-start | bytes 786440 | tf_op jit(solution)/shard_map/ppermute | solution.py:29
  243.7 4.7 %collective-permute-done.6 = bf16[1,16,8,1024]{3,1,2,0:T(8,128)(2,1)S(1)} collective-permute-done((bf16[1,16,8,1024]{3,1,2,0:T(8,128)(2,1)S(1)}, bf16[1,16,8,1024]{3,1,2,0:T(8,128)(2,1)S(1)}, u32[]{:S(2)}, u32[]{:S(2)}) %collective-permute-start.6) | collective-permute-done | bytes 262176 | tf_op jit(solution)/shard_map/ppermute | solution.py:28
  248.6 2.6 convolution_bitcast_fusion
  251.3 0.6 pad_slice_fusion.4
  251.9 0.7 pad.32
  254.2 1.9 fusion.6
  256.1 1.9 log_multiply_fusion
  258.0 1.5 mul.40
  259.5 4.1 %copy.18 = f32[16,32,1024]{2,0,1:T(8,128)} copy(f32[16,32,1024]{2,1,0:T(8,128)} %mul.40) | data formatting | bytes 4194304 | tf_op jit(solution)/shard_map/mul | solution.py:130
  263.6 48.8 %reduce-scatter.5.cloned.1.call-done = f32[16,32,128]{2,0,1:T(8,128)} async-done(((f32[16,32,1024]{2,0,1:T(8,128)}), f32[16,32,128]{2,0,1:T(8,128)}) %reduce-scatter.5.cloned.1.call-update) | async-done | bytes 262160 | tf_op jit(solution)/shard_map/reduce_scatter | solution.py:131
  312.5 1.1 exponential_multiply_fusion
  313.6 0.8 copy.19
  (62 shorter events, 7.5 us)
Async XLA Ops:
  6.5 44.8 %all-gather.3.cloned.1.call-start = ((), (), s32[]{:S(2)}) async-start(), calls=%async_computation.2 | async-start | bytes 1179648 | tf_op jit(solution)/shard_map/all_gather | solution.py:119
  8.3 153.6 %reduce-scatter.3.cloned.1.call-start = ((), (), s32[]{:S(2)}) async-start(), calls=%async_computation.3 | async-start | bytes 2359296 | tf_op jit(solution)/shard_map/reduce_scatter | solution.py:131
  16.3 47.5 %copy-start.3 = (pred[17,256,128]{2,1,0:T(32,128)(4,1)}, pred[17,256,128]{2,1,0:T(32,128)(4,1)S(1)}, u32[]{:S(2)}) copy-start(pred[17,256,128]{2,1,0:T(32,128)(4,1)S(1)} %iota_compare_fusion) | copy-start | bytes 1671172
  53.7 13.4 %collective-permute-start = (bf16[1,16,8,1024]{3,1,2,0:T(8,128)(2,1)S(1)}, bf16[1,16,8,1024]{3,1,2,0:T(8,128)(2,1)S(1)}, u32[]{:S(2)}, u32[]{:S(2)}) collective-permute-start(bf16[1,16,8,1024]{3,1,2,0:T(8,128)(2,1)S(1)} %get-tuple-element.13), channel_id=1, source_target_pairs={{0,1},{1,2},{2,3},{3,4},{4,5},{5,6},{6,7},{7,8},{8,9},{9,10},{10,1... | collective-permute-start | bytes 786440 | tf_op jit(solution)/shard_map/ppermute | solution.py:28
  55.6 11.5 %collective-permute-start.1 = (bf16[1,16,8,1024]{3,1,2,0:T(8,128)(2,1)S(1)}, bf16[1,16,8,1024]{3,1,2,0:T(8,128)(2,1)S(1)}, u32[]{:S(2)}, u32[]{:S(2)}) collective-permute-start(bf16[1,16,8,1024]{3,1,2,0:T(8,128)(2,1)S(1)} %get-tuple-element.14), channel_id=1, source_target_pairs={{1,0},{2,1},{3,2},{4,3},{5,4},{6,5},{7,6},{8,7},{9,8},{10,9},{11,1... | collective-permute-start | bytes 786440 | tf_op jit(solution)/shard_map/ppermute | solution.py:29
  62.6 4.7 %copy-start.9 = (f32[48,32]{1,0:T(8,128)}, f32[48,32]{1,0:T(8,128)S(1)}, u32[]{:S(2)}) copy-start(f32[48,32]{1,0:T(8,128)S(1)} %get-tuple-element.6) | copy-start | bytes 18436
  62.6 35.9 %copy-start.7 = (f32[48,32]{1,0:T(8,128)}, f32[48,32]{1,0:T(8,128)S(1)}, u32[]{:S(2)}) copy-start(f32[48,32]{1,0:T(8,128)S(1)} %get-tuple-element.5) | copy-start | bytes 18436
  76.1 1.9 copy-start
  80.0 13.0 %copy-start.4 = (pred[17,256,128]{2,1,0:T(32,128)(4,1)S(1)}, pred[17,256,128]{2,1,0:T(32,128)(4,1)}, u32[]{:S(2)}) copy-start(pred[17,256,128]{2,1,0:T(32,128)(4,1)} %copy-done.3) | copy-start | bytes 1671172
  83.7 13.7 %collective-permute-start.2 = (bf16[1,16,8,1024]{3,1,2,0:T(8,128)(2,1)}, bf16[1,16,8,1024]{3,1,2,0:T(8,128)(2,1)S(1)}, u32[]{:S(2)}, u32[]{:S(2)}) collective-permute-start(bf16[1,16,8,1024]{3,1,2,0:T(8,128)(2,1)} %get-tuple-element.11), channel_id=1, source_target_pairs={{0,1},{1,2},{2,3},{3,4},{4,5},{5,6},{6,7},{7,8},{8,9},{9,10},{10,1... | collective-permute-start | bytes 786440 | tf_op jit(solution)/shard_map/ppermute | solution.py:28
  85.7 11.7 %collective-permute-start.3 = (bf16[1,16,8,1024]{3,1,2,0:T(8,128)(2,1)}, bf16[1,16,8,1024]{3,1,2,0:T(8,128)(2,1)}, u32[]{:S(2)}, u32[]{:S(2)}) collective-permute-start(bf16[1,16,8,1024]{3,1,2,0:T(8,128)(2,1)} %get-tuple-element.12), channel_id=1, source_target_pairs={{1,0},{2,1},{3,2},{4,3},{5,4},{6,5},{7,6},{8,7},{9,8},{10,9},{11,1... | collective-permute-start | bytes 786440 | tf_op jit(solution)/shard_map/ppermute | solution.py:29
  94.2 11.4 %copy-start.5 = (f32[1,256,128]{2,0,1:T(1,128)}, f32[1,256,128]{2,0,1:T(1,128)S(1)}, u32[]{:S(2)}) copy-start(f32[1,256,128]{2,0,1:T(1,128)S(1)} %fusion) | copy-start | bytes 393220
  113.1 48.8 %copy-start.1 = (f32[16,32,128]{2,1,0:T(8,128)S(1)}, f32[16,32,128]{2,1,0:T(8,128)}, u32[]{:S(2)}) copy-start(f32[16,32,128]{2,1,0:T(8,128)} %param.6) | copy-start | bytes 786436
  113.1 90.7 %all-gather.5.cloned.1.call-start = ((), (), s32[]{:S(2)}) async-start(), calls=%async_computation.4 | async-start | bytes 1179648 | tf_op jit(solution)/shard_map/all_gather | solution.py:119
  163.7 148.7 %reduce-scatter.5.cloned.1.call-start = ((), (), s32[]{:S(2)}) async-start(), calls=%async_computation.5 | async-start | bytes 2359296 | tf_op jit(solution)/shard_map/reduce_scatter | solution.py:131
  206.0 13.7 %copy-start.10 = (f32[48,32]{1,0:T(8,128)S(1)}, f32[48,32]{1,0:T(8,128)}, u32[]{:S(2)}) copy-start(f32[48,32]{1,0:T(8,128)} %copy-done.9) | copy-start | bytes 18436
  206.1 13.4 %collective-permute-start.4 = (bf16[1,16,8,1024]{3,1,2,0:T(8,128)(2,1)S(1)}, bf16[1,16,8,1024]{3,1,2,0:T(8,128)(2,1)S(1)}, u32[]{:S(2)}, u32[]{:S(2)}) collective-permute-start(bf16[1,16,8,1024]{3,1,2,0:T(8,128)(2,1)S(1)} %get-tuple-element.9), channel_id=1, source_target_pairs={{0,1},{1,2},{2,3},{3,4},{4,5},{5,6},{6,7},{7,8},{8,9},{9,10},{10,1... | collective-permute-start | bytes 786440 | tf_op jit(solution)/shard_map/ppermute | solution.py:28
  208.0 11.5 %collective-permute-start.5 = (bf16[1,16,8,1024]{3,1,2,0:T(8,128)(2,1)S(1)}, bf16[1,16,8,1024]{3,1,2,0:T(8,128)(2,1)S(1)}, u32[]{:S(2)}, u32[]{:S(2)}) collective-permute-start(bf16[1,16,8,1024]{3,1,2,0:T(8,128)(2,1)S(1)} %get-tuple-element.10), channel_id=1, source_target_pairs={{1,0},{2,1},{3,2},{4,3},{5,4},{6,5},{7,6},{8,7},{9,8},{10,9},{11,1... | collective-permute-start | bytes 786440 | tf_op jit(solution)/shard_map/ppermute | solution.py:29
  234.9 13.8 %copy-start.8 = (f32[48,32]{1,0:T(8,128)S(1)}, f32[48,32]{1,0:T(8,128)}, u32[]{:S(2)}) copy-start(f32[48,32]{1,0:T(8,128)} %copy-done.7) | copy-start | bytes 18436
  234.9 13.5 %collective-permute-start.6 = (bf16[1,16,8,1024]{3,1,2,0:T(8,128)(2,1)S(1)}, bf16[1,16,8,1024]{3,1,2,0:T(8,128)(2,1)S(1)}, u32[]{:S(2)}, u32[]{:S(2)}) collective-permute-start(bf16[1,16,8,1024]{3,1,2,0:T(8,128)(2,1)S(1)} %get-tuple-element.7), channel_id=1, source_target_pairs={{0,1},{1,2},{2,3},{3,4},{4,5},{5,6},{6,7},{7,8},{8,9},{9,10},{10,1... | collective-permute-start | bytes 786440 | tf_op jit(solution)/shard_map/ppermute | solution.py:28
  236.9 11.5 %collective-permute-start.7 = (bf16[1,16,8,1024]{3,1,2,0:T(8,128)(2,1)S(1)}, bf16[1,16,8,1024]{3,1,2,0:T(8,128)(2,1)S(1)}, u32[]{:S(2)}, u32[]{:S(2)}) collective-permute-start(bf16[1,16,8,1024]{3,1,2,0:T(8,128)(2,1)S(1)} %get-tuple-element.8), channel_id=1, source_target_pairs={{1,0},{2,1},{3,2},{4,3},{5,4},{6,5},{7,6},{8,7},{9,8},{10,9},{11,1... | collective-permute-start | bytes 786440 | tf_op jit(solution)/shard_map/ppermute | solution.py:29
  253.3 0.9 copy-start.6
  263.6 48.9 %copy-start.2 = (f32[16,32,128]{2,0,1:T(8,128)S(1)}, f32[16,32,128]{2,0,1:T(8,128)}, u32[]{:S(2)}) copy-start(f32[16,32,128]{2,0,1:T(8,128)} %reduce-scatter.3.cloned.1.call-done) | copy-start | bytes 786436
Sparse Core Ops, SparseCore 0:
  9.1 42.2 all-gather.2
  113.2 48.6 reduce-scatter.2
  163.8 39.9 all-gather.4
  263.8 48.6 reduce-scatter.4
where the time goes:
time: 326 us; the launch traced here: 321 us
  waiting for transfers between devices  172 us (53%)
  matrix products  39.7 us (12%)
  starting transfers between devices  35 us (11%)
  local copies, waits for them, and re-layouts  30.2 us (9%)
  blocking collectives  16.1 us (5%)
  between operations  15.2 us (5%)
  other arithmetic  13.2 us (4%)
    reduce_scatter x2, waiting for transfers between devices, body(): lax.psum_scatter(log_term, 'view', scatter_dimension=2, tiled=True)  80.9 us
    all_gather x2, waiting for transfers between devices, body(): lax.all_gather(current.astype(jnp.bfloat16), 'view', axis=2, tiled=True)  74.9 us
    ppermute x4, starting transfers between devices, padded(): after = lax.ppermute(leading, axis, down)  26.8 us
    psum x1, blocking collectives, body(): view_count = lax.psum(coverage[0, 0], 'view').astype(jnp.float32)  16.1 us
    ppermute x4, waiting for transfers between devices, padded(): before = lax.ppermute(last, axis, up)  16 us
    mul x4, local copies, waits for them, and re-layouts, body(): covered[:, None, None, None] * jnp.log(updated_estimate)  11.3 us
    dot_general x4, matrix products, lateral_rows(): jnp.einsum('cnkw,ckr->cnrw', widened_ratio, banded_kernels[0], precision=...  10.4 us
    ppermute x4, starting transfers between devices, padded(): before = lax.ppermute(last, axis, up)  7.81 us
  transfers between devices with their start and end apart: 12, of which 8 were waited for; matrix products, arithmetic and copies ran while one was open for 3% of the time, Pallas kernels for 0%

commit v1 on v0

v1 whole, which is shorter than its diff:
```python
import functools

import jax
import jax.numpy as jnp
from jax import lax
from jax.experimental import pallas as pl
from jax.experimental.pallas import tpu as pltpu
from jax.sharding import PartitionSpec as P

MESH = pl.DeviceIdType.MESH
F32, BF16 = jnp.float32, jnp.bfloat16
SHIFT, ITERS = 4, 2
NZ, TY, BX, NV, NT = 16, 32, 128, 8, 32
KZ, KXY = 65, 9
EXACT = lax.Precision.HIGHEST


def lanes(shape):
    return lax.broadcasted_iota(jnp.int32, shape, len(shape) - 1)


def toeplitz(row, count):
    x = jnp.broadcast_to(row, (count, row.shape[-1]))
    r = lax.broadcasted_iota(jnp.int32, x.shape, 0)
    bit = 1
    while bit < count:
        x = jnp.where((r & bit) != 0, pltpu.roll(x, bit, 1), x)
        bit *= 2
    return x


def kernel(
    est, meas, pz, pxy, offs, cov, out,
    mbuf, pb, fld, hr, hl, sr, sl, mm, mq, mu, md, sq, su, sd,
    rz, ry, az, ay, wf, wb, xf, xb, bl, rt, acc, cur,
    loc, ps, pr, fs, fr, ms, mr,
):
    v, t = lax.axis_index("view"), lax.axis_index("tile")
    has_up, has_down = t > 0, t < NT - 1
    has_left, has_right = v > 0, v < NV - 1

    def remote(src, dst, send, recv, dv, dt):
        return pltpu.make_async_remote_copy(
            src_ref=src, dst_ref=dst, send_sem=send, recv_sem=recv, device_id=(dv, dt), device_id_type=MESH
        )

    own_cols = pl.ds(pl.multiple_of(v * BX, BX), BX)
    get_all = pltpu.make_async_copy(meas.at[0], mbuf, loc.at[0])
    get_own = pltpu.make_async_copy(meas.at[0, :, :, own_cols], mm.at[v], loc.at[1])
    get_all.start()
    get_own.start()

    barrier = pltpu.get_barrier_semaphore()
    tiles = (t, lax.rem(t + 1, NT), lax.rem(t + NT - 1, NT))
    for s in range(NV):
        for k, dt in enumerate(tiles):
            if s or k:
                pl.semaphore_signal(barrier, inc=1, device_id=(lax.rem(v + s, NV), dt), device_id_type=MESH)

    lane1 = lanes((1, BX))
    zero1 = jnp.zeros((1, BX), F32)

    def taps(values, places):
        row = zero1
        for value, place in zip(values, places):
            row = jnp.where(lane1 == place, value, row)
        return row

    z_taps = [pz[0, i] for i in range(KZ)]
    y_taps = [pxy[0, 0, i] for i in range(KXY)]
    x_taps = [pxy[0, 1, i] for i in range(KXY)]
    oy, ox = offs[0, 0], offs[0, 1]

    def normal(values):
        return jnp.full((1, BX), functools.reduce(lambda a, b: a + b, values), F32)

    zn, yn, xn = normal(z_taps), normal(y_taps), normal(x_taps)
    rows = [
        taps(z_taps, range(KZ)) / zn,
        taps(z_taps, [KZ - 1 - i for i in range(KZ)]) / zn,
        taps(y_taps, [i + SHIFT + oy for i in range(KXY)]) / yn,
        taps(y_taps, [16 - (i + SHIFT + oy) for i in range(KXY)]) / yn,
        taps(x_taps, [4 - i - ox for i in range(KXY)]) / xn,
        taps(x_taps, [132 - i - ox for i in range(KXY)]) / xn,
        taps(x_taps, [i - 4 + ox for i in range(KXY)]) / xn,
        taps(x_taps, [i + 124 + ox for i in range(KXY)]) / xn,
        jnp.full((1, BX), cov[0, 0].astype(F32)),
    ]
    for i, row in enumerate(rows):
        pb[v, i : i + 1, :] = row
    pb[v, len(rows) :, :] = jnp.zeros((16 - len(rows), BX), F32)

    pl.semaphore_wait(barrier, 3 * NV - 1)

    for s in range(1, NV):
        d = lax.rem(v + s, NV)
        remote(pb.at[v], pb.at[v], ps.at[d], pr.at[v], d, t).start()

    plane_lane = lanes((TY, BX))
    wide_lane = lanes((2 * TY, BX))

    def field_copies(it):
        f = fld.at[it]
        up, down, left, right = t - 1, t + 1, v - 1, v + 1
        top, low = pl.ds(0, 16), pl.ds(16, 16)
        main = pl.ds(0, BX)
        specs = [
            (has_up, has_down, f.at[:, pl.ds(16, 16), main], f.at[:, pl.ds(48, 16), main], v, up),
            (has_down, has_up, f.at[:, pl.ds(32, 16), main], f.at[:, pl.ds(0, 16), main], v, down),
        ]
        for ok_to, ok_from, s, h, dv in ((has_left, has_right, sr, hr, left), (has_right, has_left, sl, hl, right)):
            specs += [
                (ok_to, ok_from, s.at[it], h.at[it, :, pl.ds(16, 32)], dv, t),
                (ok_to & has_up, ok_from & has_down, s.at[it, :, top], h.at[it, :, pl.ds(48, 16)], dv, up),
                (ok_to & has_down, ok_from & has_up, s.at[it, :, low], h.at[it, :, pl.ds(0, 16)], dv, down),
            ]
        return [
            (ok_to, ok_from, dst, remote(src, dst, fs.at[it, i], fr.at[it, i], dv, dt))
            for i, (ok_to, ok_from, src, dst, dv, dt) in enumerate(specs)
        ]

    def send_field(it, source):
        for z in range(NZ):
            fld[it, z, 16:48, 0:BX] = source[z].astype(BF16)
        copies = field_copies(it)
        for ok_to, _, _, copy in copies[:2]:
            pl.when(ok_to)(copy.start)
        for q in range(2):
            head = jnp.zeros((TY, BX), F32)
            tail = jnp.zeros((TY, BX), F32)
            for k in range(8):
                rolled = source[8 * q + k]
                if k:
                    rolled = pltpu.roll(rolled, 16 * k, 1)
                head = jnp.where(plane_lane // 16 == k, rolled, head)
                tail = jnp.where(plane_lane // 16 == (k + 7) % 8, rolled, tail)
            sr[it, q] = head.astype(BF16)
            sl[it, q] = tail.astype(BF16)
        for ok_to, _, _, copy in copies[2:]:
            pl.when(ok_to)(copy.start)

    def receive_field(it):
        for _, ok_from, dst, copy in field_copies(it):
            pl.when(ok_from)(copy.wait_recv)

            @pl.when(jnp.logical_not(ok_from))
            def _():
                dst[...] = jnp.zeros(dst.shape, BF16)

        for q in range(2):
            right = hr[it, q].astype(F32)
            left = hl[it, q].astype(F32)
            for k in range(8):
                both = jnp.where(wide_lane // 16 == k, right, left)
                if k:
                    both = pltpu.roll(both, BX - 16 * k, 1)
                both = jnp.where((wide_lane < 16) | (wide_lane >= 112), both, 0.0)
                fld[it, 8 * q + k, :, BX:] = both.astype(BF16)

    send_field(0, est)

    get_all.wait()
    for s in range(1, NV):
        d = lax.rem(v + s, NV)
        cols = pl.ds(pl.multiple_of(d * BX, BX), BX)
        remote(mbuf.at[:, :, cols], mm.at[v], ms.at[0, d], mr.at[0, v], d, t).start()

    def pack_measured(s, carry):
        d = lax.rem(v + s, NV)
        here = pl.ds(pl.multiple_of(d * BX, BX), BX)
        after = pl.ds(pl.multiple_of(jnp.minimum(d + 1, NV - 1) * BX, BX), BX)
        before = pl.ds(pl.multiple_of(jnp.maximum(d - 1, 0) * BX, BX), BX)
        take_after = (plane_lane < 8) & (d < NV - 1)
        take_before = (plane_lane >= 120) & (d > 0)
        corners = []
        for q in range(2):
            packed = jnp.zeros((TY, BX), F32)
            for k in range(8):
                z = 8 * q + k
                edge = jnp.where(
                    take_after, mbuf[z, :, after].astype(F32),
                    jnp.where(take_before, mbuf[z, :, before].astype(F32), 0.0),
                )
                packed = packed + (pltpu.roll(edge, 16 * k, 1) if k else edge)
            sq[d, q] = packed.astype(BF16)
            corners.append(packed)
        for p in range(NZ // 2):
            a = mbuf[2 * p, :, here].astype(F32)
            b = mbuf[2 * p + 1, :, here].astype(F32)
            sd[d, p] = jnp.concatenate([a[0:8], b[0:8]], axis=0).astype(BF16)
            su[d, p] = jnp.concatenate([a[24:32], b[24:32]], axis=0).astype(BF16)
        sd[d, 8] = jnp.concatenate([corners[0][0:8], corners[1][0:8]], axis=0).astype(BF16)
        su[d, 8] = jnp.concatenate([corners[0][24:32], corners[1][24:32]], axis=0).astype(BF16)

        @pl.when(d != v)
        def _():
            remote(sq.at[d], mq.at[v], ms.at[1, d], mr.at[1, v], d, t).start()

        @pl.when(has_down)
        def _():
            remote(su.at[d], mu.at[v], ms.at[2, d], mr.at[2, v], d, t + 1).start()

        @pl.when(has_up)
        def _():
            remote(sd.at[d], md.at[v], ms.at[3, d], mr.at[3, v], d, t - 1).start()

        return carry

    lax.fori_loop(0, NV, pack_measured, 0)
    mq[v] = sq[v]

    for s in range(1, NV):
        u = lax.rem(v + s, NV)
        remote(pb.at[u], pb.at[u], ps.at[u], pr.at[u], u, t).wait_recv()

    def small_bands(u, carry):
        z16 = pl.ds(pl.multiple_of(u * 16, 16), 16)
        for half in range(2):
            rz[half, z16, :] = toeplitz(pb[u, half : half + 1, :], 16)
            ry[half, z16, :] = toeplitz(pb[u, 2 + half : 3 + half, :], 16)
        for source, target in ((4, xf), (6, xb)):
            row = jnp.concatenate([pb[u, source : source + 1, :], pb[u, source + 1 : source + 2, :]], axis=1)
            base = toeplitz(row, 16)
            width = target.shape[-1]
            for g in range(16):
                part = (pltpu.roll(base, 16 * g, 1) if g else base)[:, :width]
                high = part.astype(BF16)
                target[0, u, 16 * g : 16 * g + 16, :] = high
                target[1, u, 16 * g : 16 * g + 16, :] = (part - high.astype(F32)).astype(BF16)
        return carry

    lax.fori_loop(0, NV, small_bands, 0)
    m = lax.broadcasted_iota(jnp.int32, (BX, 512), 0)
    n = lanes((BX, 512))
    spread_z = (m == n // 32 + 32).astype(F32)
    spread_y = (m == n % 32).astype(F32)
    for half in range(2):
        az[half] = jnp.dot(rz[half], spread_z, precision=EXACT, preferred_element_type=F32)
        ay[half] = jnp.dot(ry[half], spread_y, precision=EXACT, preferred_element_type=F32)

    def depth_rows(u, carry):
        z16 = pl.ds(pl.multiple_of(u * 16, 16), 16)
        for half, target in enumerate((wf, wb)):
            a = az[half, z16, :]
            y = ay[half, z16, :]
            for z in range(NZ):
                target[u, 16 * z : 16 * z + 16, :] = (a[z : z + 1] * y).astype(BF16)
        return carry

    lax.fori_loop(0, NV, depth_rows, 0)

    def forward(it):
        receive_field(it)

        def view(u, carry):
            for c in range(3):
                chunk = fld[it, :, 16 * c : 16 * c + 32, :].reshape(512, 256)
                zy = jnp.dot(wf[u], chunk, preferred_element_type=F32).astype(BF16)
                full = jnp.dot(zy, xf[0, u], preferred_element_type=F32)
                full = full + jnp.dot(zy, xf[1, u], preferred_element_type=F32)
                bl[u, :, 16 * c : 16 * c + 16, :] = full.reshape(NZ, 16, 256)
            return carry

        lax.fori_loop(0, NV, view, 0)

    ext_lane = lanes((48, BX))

    def wait_measured(u):
        @pl.when(u != v)
        def _():
            remote(mbuf.at[:, :, pl.ds(0, BX)], mm.at[u], ms.at[0, u], mr.at[0, u], u, t).wait_recv()
            remote(sq.at[u], mq.at[u], ms.at[1, u], mr.at[1, u], u, t).wait_recv()

        @pl.when(has_up)
        def _():
            remote(su.at[u], mu.at[u], ms.at[2, u], mr.at[2, u], u, t).wait_recv()

        @pl.when(has_down)
        def _():
            remote(sd.at[u], md.at[u], ms.at[3, u], mr.at[3, u], u, t).wait_recv()

    @pl.when(jnp.logical_not(has_up))
    def _():
        mu[...] = jnp.zeros(mu.shape, BF16)

    @pl.when(jnp.logical_not(has_down))
    def _():
        md[...] = jnp.zeros(md.shape, BF16)

    def ratio(values, blurred):
        return jnp.where(values > 0, values / blurred, 0.0).astype(BF16)

    def backward(first):
        acc[...] = jnp.zeros(acc.shape, F32)

        def view(s, carry):
            u = lax.rem(v + s, NV)
            if first:
                wait_measured(u)
            cu, cd = mu[u, 8].astype(F32), md[u, 8].astype(F32)
            for q in range(2):
                rows8 = slice(8 * q, 8 * q + 8)
                edge = jnp.concatenate([cu[rows8], mq[u, q].astype(F32), cd[rows8]], axis=0)
                for k in range(8):
                    z = 8 * q + k
                    side = pltpu.roll(edge, BX - 16 * k, 1) if k else edge
                    side = jnp.where((ext_lane < 8) | (ext_lane >= 120), side, 0.0)
                    rt[z, :, BX:] = ratio(side, bl[u, z, :, BX:])
                    r = slice(8 * (z % 2), 8 * (z % 2) + 8)
                    main = jnp.concatenate(
                        [mu[u, z // 2].astype(F32)[r], mm[u, z].astype(F32), md[u, z // 2].astype(F32)[r]], axis=0
                    )
                    rt[z, :, :BX] = ratio(main, bl[u, z, :, :BX])
            weight = pb[u, 8:9, :]
            for c in range(2):
                chunk = rt[:, 16 * c : 16 * c + 32, :].reshape(512, 256)
                zy = jnp.dot(wb[u], chunk, preferred_element_type=F32)
                high = zy.astype(BF16)
                low = (zy - high.astype(F32)).astype(BF16)
                back = jnp.dot(high, xb[0, u], preferred_element_type=F32)
                back = back + jnp.dot(low, xb[0, u], preferred_element_type=F32)
                back = back + jnp.dot(high, xb[1, u], preferred_element_type=F32)
                acc[:, 16 * c : 16 * c + 16, :] += (weight * jnp.log(back)).reshape(NZ, 16, BX)
            return carry

        lax.fori_loop(0, NV, view, 0)

    count = pb[0, 8:9, :]
    for u in range(1, NV):
        count = count + pb[u, 8:9, :]

    get_own.wait()
    forward(0)
    backward(True)
    for z in range(NZ):
        cur[z] = est[z] * jnp.exp(acc[z] / count)
    send_field(1, cur)
    forward(1)
    backward(False)
    for z in range(NZ):
        out[z] = cur[z] * jnp.exp(acc[z] / count)

    for it in range(ITERS):
        for ok_to, _, _, copy in field_copies(it):
            pl.when(ok_to)(copy.wait_send)

    def drain(s, carry):
        d = lax.rem(v + s, NV)

        @pl.when(d != v)
        def _():
            remote(pb.at[v], pb.at[v], ps.at[d], pr.at[d], d, t).wait_send()
            remote(mbuf.at[:, :, pl.ds(0, BX)], mm.at[v], ms.at[0, d], mr.at[0, d], d, t).wait_send()
            remote(sq.at[d], mq.at[v], ms.at[1, d], mr.at[1, d], d, t).wait_send()

        @pl.when(has_down)
        def _():
            remote(su.at[d], mu.at[v], ms.at[2, d], mr.at[2, d], d, t).wait_send()

        @pl.when(has_up)
        def _():
            remote(sd.at[d], md.at[v], ms.at[3, d], mr.at[3, d], d, t).wait_send()

        return carry

    lax.fori_loop(0, NV, drain, 0)


def body(estimate, measured, psf_z, psf_xy, offsets, coverage):
    vmem = pl.BlockSpec(memory_space=pltpu.VMEM)
    smem = pl.BlockSpec(memory_space=pltpu.SMEM)
    scratch = [
        ((NZ, TY, NV * BX), BF16), ((NV, 16, BX), F32),
        ((2, NZ, 64, 256), BF16), ((2, 2, 64, BX), BF16), ((2, 2, 64, BX), BF16),
        ((2, 2, TY, BX), BF16), ((2, 2, TY, BX), BF16),
        ((NV, NZ, TY, BX), BF16), ((NV, 2, TY, BX), BF16), ((NV, 9, 16, BX), BF16), ((NV, 9, 16, BX), BF16),
        ((NV, 2, TY, BX), BF16), ((NV, 9, 16, BX), BF16), ((NV, 9, 16, BX), BF16),
        ((2, 128, BX), F32), ((2, 128, BX), F32), ((2, 128, 512), F32), ((2, 128, 512), F32),
        ((NV, 256, 512), BF16), ((NV, 256, 512), BF16), ((2, NV, 256, 256), BF16), ((2, NV, 256, BX), BF16),
        ((NV, NZ, 48, 256), F32), ((NZ, 48, 256), BF16), ((NZ, TY, BX), F32), ((NZ, TY, BX), F32),
    ]
    dma = pltpu.SemaphoreType.DMA
    return pl.pallas_call(
        kernel,
        out_shape=jax.ShapeDtypeStruct(estimate.shape, F32),
        in_specs=[vmem, pl.BlockSpec(memory_space=pl.ANY), smem, smem, smem, smem],
        out_specs=vmem,
        scratch_shapes=[pltpu.VMEM(s, d) for s, d in scratch]
        + [dma((2,)), dma((NV,)), dma((NV,)), dma((2, 8)), dma((2, 8)), dma((4, NV)), dma((4, NV))],
        compiler_params=pltpu.CompilerParams(
            collective_id=0, has_side_effects=True, vmem_limit_bytes=48 * 1024 * 1024
        ),
    )(estimate, measured, psf_z, psf_xy, offsets, coverage)


def solution(mesh):
    placed = (
        P(None, "tile", "view"),
        P("view", None, "tile", None),
        P("view", None),
        P("view", None, None),
        P("view", None),
        P("view", "tile"),
    )
    return jax.shard_map(
        body, mesh=mesh, in_specs=placed, out_specs=P(None, "tile", "view"), check_vma=False
    )
```

time: 326 us -> 66.8 us (0.20); the launches traced: 321 us -> 66.5 us
  waiting for transfers between devices: 172 us -> 0 us
  Pallas kernels: 0 us -> 62.2 us
  matrix products: 39.7 us -> 0 us
  starting transfers between devices: 35 us -> 0 us
  local copies, waits for them, and re-layouts: 30.2 us -> 3.53 us
  blocking collectives: 16.1 us -> 0 us
  between operations: 15.2 us -> 0.72 us
  other arithmetic: 13.2 us -> 0 us
    reduce_scatter x2 -> x0, waiting for transfers between devices: 80.9 us -> none  [body(): lax.psum_scatter(log_term, 'view', scatter_dimension=2, tiled=True)]
    all_gather x2 -> x0, waiting for transfers between devices: 74.9 us -> none  [body(): lax.all_gather(current.astype(jnp.bfloat16), 'view', axis=2, tiled=True)]
    pallas_call x0 -> x1, Pallas kernels: none -> 62.2 us  [body(): pl.pallas_call(kernel, out_shape=jax.ShapeDtypeStruct(estimate.shape, F32...]
    dot_general x21 -> x0, matrix products: 39.7 us -> none  [the longest x4 10.4 us: lateral_rows(): jnp.einsum('cnkw,ckr->cnrw', widened_ratio, banded_kernels[0], precision=...]
    ppermute x8 -> x0, starting transfers between devices: 34.7 us -> none  [the longest x4 26.8 us: padded(): after = lax.ppermute(leading, axis, down)]
    psum x1 -> x0, blocking collectives: 16.1 us -> none  [body(): view_count = lax.psum(coverage[0, 0], 'view').astype(jnp.float32)]
    ppermute x8 -> x0, waiting for transfers between devices: 16 us -> none  [the longest x4 16 us: padded(): before = lax.ppermute(last, axis, up)]
    mul x5 -> x0, local copies, waits for them, and re-layouts: 12.1 us -> none  [the longest x4 11.3 us: body(): covered[:, None, None, None] * jnp.log(updated_estimate)]
  transfers between devices with their start and end apart: 12 -> 0, of which waited for: 8 -> 0; matrix products, arithmetic and copies ran while one was open for 3% -> 0% of each run, Pallas kernels for 0% -> 0%
where the time goes in v1:
time: 66.8 us; the launch traced here: 66.5 us
  Pallas kernels  62.2 us (93%)
  local copies, waits for them, and re-layouts  3.53 us (5%)
  between operations  0.72 us (1%)
    pallas_call x1, Pallas kernels, body(): pl.pallas_call(kernel, out_shape=jax.ShapeDtypeStruct(estimate.shape, F32...  62.2 us
    unnamed x11, local copies, waits for them, and re-layouts  3.53 us

profile of v1, /device:TPU:48, one launch (start us, length us, event | category | flops | bytes accessed | tf_op | source)
XLA Modules:
  0.0 66.5 jit_solution(6193436545962696350)
XLA Ops:
  0.0 0.0 copy-start.2
  0.0 0.0 copy-start.3
  0.7 0.0 copy-done.2
  0.7 0.0 copy-done.3
  0.7 0.0 copy-start
  0.7 1.2 %copy-done = bf16[1,16,32,1024]{3,2,1,0:T(8,128)(2,1)S(1)} copy-done((bf16[1,16,32,1024]{3,2,1,0:T(8,128)(2,1)S(1)}, bf16[1,16,32,1024]{3,2,1,0:T(8,128)(2,1)}, u32[]{:S(2)}) %copy-start) | copy-done | bytes 1048600
  1.9 0.0 copy-start.1
  1.9 0.9 %copy-done.1 = f32[16,32,128]{2,1,0:T(8,128)S(1)} copy-done((f32[16,32,128]{2,1,0:T(8,128)S(1)}, f32[16,32,128]{2,1,0:T(8,128)}, u32[]{:S(2)}) %copy-start.1) | copy-done | bytes 262168
  2.9 0.0 copy-start.4
  2.9 0.7 copy-done.4
  3.5 62.2 %shard_map.64 = f32[16,32,128]{2,1,0:T(8,128)S(1)} custom-call(f32[16,32,128]{2,1,0:T(8,128)S(1)} %copy-done.1, bf16[1,16,32,1024]{3,2,1,0:T(8,128)(2,1)S(1)} %copy-done, f32[1,65]{1,0:T(1,128)S(1)} %copy-done.3, f32[1,2,9]{2,1,0:T(2,128)S(1)} %copy-done.2, s32[1,2]{1,0:T(1,128)S(1)} %copy-done.4, s32[1,1]{1,0:T(1,128)S(6)} %copy.8.cov), custom_call_target="tpu_custom_call" | custom-call | tf_op jit(solution)/shard_map/pallas_call | solution.py:383
  65.8 0.7 %copy.9 = f32[16,32,128]{2,1,0:T(8,128)} copy(f32[16,32,128]{2,1,0:T(8,128)S(1)} %shard_map.64) | data formatting | bytes 524288
Async XLA Ops:
  0.0 0.7 %copy-start.2 = (f32[1,2,9]{2,1,0:T(2,128)S(1)}, f32[1,2,9]{2,1,0:T(2,128)}, u32[]{:S(2)}) copy-start(f32[1,2,9]{2,1,0:T(2,128)} %pxy.1) | copy-start | bytes 220
  0.0 0.7 %copy-start.3 = (f32[1,65]{1,0:T(1,128)S(1)}, f32[1,65]{1,0:T(1,128)}, u32[]{:S(2)}) copy-start(f32[1,65]{1,0:T(1,128)} %pz.1) | copy-start | bytes 784
  0.7 1.2 %copy-start = (bf16[1,16,32,1024]{3,2,1,0:T(8,128)(2,1)S(1)}, bf16[1,16,32,1024]{3,2,1,0:T(8,128)(2,1)}, u32[]{:S(2)}) copy-start(bf16[1,16,32,1024]{3,2,1,0:T(8,128)(2,1)} %meas.1) | copy-start | bytes 3145732
  1.9 0.9 %copy-start.1 = (f32[16,32,128]{2,1,0:T(8,128)S(1)}, f32[16,32,128]{2,1,0:T(8,128)}, u32[]{:S(2)}) copy-start(f32[16,32,128]{2,1,0:T(8,128)} %est.1) | copy-start | bytes 786436
  2.9 0.7 copy-start.4

commit v2 on v1

v2 whole, which is shorter than its diff:
```python
import functools

import jax
import jax.numpy as jnp
from jax import lax
from jax.experimental import pallas as pl
from jax.experimental.pallas import tpu as pltpu
from jax.sharding import PartitionSpec as P

MESH = pl.DeviceIdType.MESH
F32, BF16 = jnp.float32, jnp.bfloat16
SHIFT, ITERS = 4, 2
NZ, TY, BX, NV, NT = 16, 32, 128, 8, 32
KZ, KXY = 65, 9
EXACT = lax.Precision.HIGHEST


def lanes(shape):
    return lax.broadcasted_iota(jnp.int32, shape, len(shape) - 1)


def toeplitz(row, count):
    x = jnp.broadcast_to(row, (count, row.shape[-1]))
    r = lax.broadcasted_iota(jnp.int32, x.shape, 0)
    bit = 1
    while bit < count:
        x = jnp.where((r & bit) != 0, pltpu.roll(x, bit, 1), x)
        bit *= 2
    return x


def kernel(
    est_hbm, meas, pz_hbm, pxy_hbm, offs_hbm, cov_hbm, out,
    est, pz, pxy, offs, cov,
    mbuf, pb, fld, hr, hl, sr, sl, mm, mq, mu, md, sq, su, sd,
    rz, ry, az, ay, wf, wb, xf, xb, bl, mext, rt, acc, cur,
    loc, ps, pr, fs, fr, ms, mr,
):
    v, t = lax.axis_index("view"), lax.axis_index("tile")
    has_up, has_down = t > 0, t < NT - 1
    has_left, has_right = v > 0, v < NV - 1

    def remote(src, dst, send, recv, dv, dt):
        return pltpu.make_async_remote_copy(
            src_ref=src, dst_ref=dst, send_sem=send, recv_sem=recv, device_id=(dv, dt), device_id_type=MESH
        )

    own_cols = pl.ds(pl.multiple_of(v * BX, BX), BX)
    get_all = pltpu.make_async_copy(meas.at[0], mbuf, loc.at[0])
    get_own = pltpu.make_async_copy(meas.at[0, :, :, own_cols], mm.at[v], loc.at[1])
    small = [
        pltpu.make_async_copy(src, dst, loc.at[2 + i])
        for i, (src, dst) in enumerate(
            ((pz_hbm, pz), (pxy_hbm, pxy), (offs_hbm, offs), (cov_hbm, cov), (est_hbm, est))
        )
    ]
    for copy in small:
        copy.start()
    get_all.start()
    get_own.start()

    barrier = pltpu.get_barrier_semaphore()
    up_tile, down_tile = lax.rem(t + NT - 1, NT), lax.rem(t + 1, NT)
    partners = [(lax.rem(v + s, NV), t) for s in range(1, NV)]
    partners += [(lax.rem(v + s, NV), dt) for s in (0, 1, NV - 1) for dt in (up_tile, down_tile)]
    for partner in partners:
        pl.semaphore_signal(barrier, inc=1, device_id=partner, device_id_type=MESH)
    for copy in small[:4]:
        copy.wait()

    lane1 = lanes((1, BX))
    zero1 = jnp.zeros((1, BX), F32)

    def taps(values, places):
        row = zero1
        for value, place in zip(values, places):
            row = jnp.where(lane1 == place, value, row)
        return row

    z_taps = [pz[0, i] for i in range(KZ)]
    y_taps = [pxy[0, 0, i] for i in range(KXY)]
    x_taps = [pxy[0, 1, i] for i in range(KXY)]
    oy, ox = offs[0, 0], offs[0, 1]

    def normal(values):
        return jnp.full((1, BX), functools.reduce(lambda a, b: a + b, values), F32)

    zn, yn, xn = normal(z_taps), normal(y_taps), normal(x_taps)
    rows = [
        taps(z_taps, range(KZ)) / zn,
        taps(z_taps, [KZ - 1 - i for i in range(KZ)]) / zn,
        taps(y_taps, [i + SHIFT + oy for i in range(KXY)]) / yn,
        taps(y_taps, [16 - (i + SHIFT + oy) for i in range(KXY)]) / yn,
        taps(x_taps, [4 - i - ox for i in range(KXY)]) / xn,
        taps(x_taps, [132 - i - ox for i in range(KXY)]) / xn,
        taps(x_taps, [i - 4 + ox for i in range(KXY)]) / xn,
        taps(x_taps, [i + 124 + ox for i in range(KXY)]) / xn,
        jnp.full((1, BX), cov[0, 0].astype(F32)),
    ]
    for i, row in enumerate(rows):
        pb[v, i : i + 1, :] = row
    pb[v, len(rows) :, :] = jnp.zeros((16 - len(rows), BX), F32)

    plane_lane = lanes((TY, BX))
    wide_lane = lanes((2 * TY, BX))

    def field_copies(it):
        f = fld.at[it]
        up, down, left, right = t - 1, t + 1, v - 1, v + 1
        top, low = pl.ds(0, 16), pl.ds(16, 16)
        main = pl.ds(0, BX)
        specs = [
            (has_up, has_down, f.at[:, pl.ds(16, 16), main], f.at[:, pl.ds(48, 16), main], v, up),
            (has_down, has_up, f.at[:, pl.ds(32, 16), main], f.at[:, pl.ds(0, 16), main], v, down),
        ]
        for ok_to, ok_from, s, h, dv in ((has_left, has_right, sr, hr, left), (has_right, has_left, sl, hl, right)):
            specs += [
                (ok_to, ok_from, s.at[it], h.at[it, :, pl.ds(16, 32)], dv, t),
                (ok_to & has_up, ok_from & has_down, s.at[it, :, top], h.at[it, :, pl.ds(48, 16)], dv, up),
                (ok_to & has_down, ok_from & has_up, s.at[it, :, low], h.at[it, :, pl.ds(0, 16)], dv, down),
            ]
        return [
            (ok_to, ok_from, dst, remote(src, dst, fs.at[it, i], fr.at[it, i], dv, dt))
            for i, (ok_to, ok_from, src, dst, dv, dt) in enumerate(specs)
        ]

    def pack_field(it, source):
        for z in range(NZ):
            fld[it, z, 16:48, 0:BX] = source[z].astype(BF16)
        for q in range(2):
            head = jnp.zeros((TY, BX), F32)
            tail = jnp.zeros((TY, BX), F32)
            for k in range(8):
                rolled = source[8 * q + k]
                if k:
                    rolled = pltpu.roll(rolled, 16 * k, 1)
                head = jnp.where(plane_lane // 16 == k, rolled, head)
                tail = jnp.where(plane_lane // 16 == (k + 7) % 8, rolled, tail)
            sr[it, q] = head.astype(BF16)
            sl[it, q] = tail.astype(BF16)

    def send_field(it):
        for ok_to, _, _, copy in field_copies(it):
            pl.when(ok_to)(copy.start)

    def receive_field(it):
        for _, ok_from, dst, copy in field_copies(it):
            pl.when(ok_from)(copy.wait_recv)

            @pl.when(jnp.logical_not(ok_from))
            def _():
                dst[...] = jnp.zeros(dst.shape, BF16)

        for q in range(2):
            right = hr[it, q].astype(F32)
            left = hl[it, q].astype(F32)
            for k in range(8):
                both = jnp.where(wide_lane // 16 == k, right, left)
                if k:
                    both = pltpu.roll(both, BX - 16 * k, 1)
                both = jnp.where((wide_lane < 16) | (wide_lane >= 112), both, 0.0)
                fld[it, 8 * q + k, :, BX:] = both.astype(BF16)

    small[4].wait()
    pack_field(0, est)
    get_all.wait()

    def pack_columns(d, carry):
        after = pl.ds(pl.multiple_of(jnp.minimum(d + 1, NV - 1) * BX, BX), BX)
        before = pl.ds(pl.multiple_of(jnp.maximum(d - 1, 0) * BX, BX), BX)
        take_after = (plane_lane < 8) & (d < NV - 1)
        take_before = (plane_lane >= 120) & (d > 0)
        for q in range(2):
            packed = jnp.zeros((TY, BX), F32)
            for k in range(8):
                z = 8 * q + k
                edge = jnp.where(
                    take_after, mbuf[z, :, after].astype(F32),
                    jnp.where(take_before, mbuf[z, :, before].astype(F32), 0.0),
                )
                packed = packed + (pltpu.roll(edge, 16 * k, 1) if k else edge)
            sq[d, q] = packed.astype(BF16)
        return carry

    lax.fori_loop(0, NV, pack_columns, 0)
    mq[v] = sq[v]

    pl.semaphore_wait(barrier, len(partners))
    for s in range(1, NV):
        d = lax.rem(v + s, NV)
        remote(pb.at[v], pb.at[v], ps.at[d], pr.at[v], d, t).start()
    send_field(0)
    for s in range(1, NV):
        d = lax.rem(v + s, NV)
        cols = pl.ds(pl.multiple_of(d * BX, BX), BX)
        remote(mbuf.at[:, :, cols], mm.at[v], ms.at[0, d], mr.at[0, v], d, t).start()
        remote(sq.at[d], mq.at[v], ms.at[1, d], mr.at[1, v], d, t).start()

    for s in range(1, NV):
        u = lax.rem(v + s, NV)
        remote(pb.at[u], pb.at[u], ps.at[u], pr.at[u], u, t).wait_recv()

    def small_bands(u, carry):
        z16 = pl.ds(pl.multiple_of(u * 16, 16), 16)
        for half in range(2):
            rz[half, z16, :] = toeplitz(pb[u, half : half + 1, :], 16)
            ry[half, z16, :] = toeplitz(pb[u, 2 + half : 3 + half, :], 16)
        for source, target in ((4, xf), (6, xb)):
            row = jnp.concatenate([pb[u, source : source + 1, :], pb[u, source + 1 : source + 2, :]], axis=1)
            base = toeplitz(row, 16)
            width = target.shape[-1]
            for g in range(16):
                part = (pltpu.roll(base, 16 * g, 1) if g else base)[:, :width]
                target[u, 16 * g : 16 * g + 16, :] = part.astype(BF16)
        return carry

    lax.fori_loop(0, NV, small_bands, 0)
    m = lax.broadcasted_iota(jnp.int32, (BX, 512), 0)
    n = lanes((BX, 512))
    spread_z = (m == n // 32 + 32).astype(F32)
    spread_y = (m == n % 32).astype(F32)
    for half in range(2):
        az[half] = jnp.dot(rz[half], spread_z, precision=EXACT, preferred_element_type=F32)
        ay[half] = jnp.dot(ry[half], spread_y, precision=EXACT, preferred_element_type=F32)

    def depth_rows(u, carry):
        z16 = pl.ds(pl.multiple_of(u * 16, 16), 16)
        for half, target in enumerate((wf, wb)):
            a = az[half, z16, :]
            y = ay[half, z16, :]
            for z in range(NZ):
                target[u, 16 * z : 16 * z + 16, :] = (a[z : z + 1] * y).astype(BF16)
        return carry

    lax.fori_loop(0, NV, depth_rows, 0)

    def blur(it, u):
        parts = []
        for c in range(3):
            chunk = fld[it, :, 16 * c : 16 * c + 32, :].reshape(512, 256)
            parts.append(jnp.dot(wf[u], chunk, preferred_element_type=F32).astype(BF16))
        return jnp.dot(jnp.concatenate(parts, axis=0), xf[u], preferred_element_type=F32)

    def relay_copies(u):
        return (
            (has_down, has_up, remote(su.at[u], mu.at[u], ms.at[2, u], mr.at[2, u], v, t + 1)),
            (has_up, has_down, remote(sd.at[u], md.at[u], ms.at[3, u], mr.at[3, u], v, t - 1)),
        )

    def relay(u):
        @pl.when(u != v)
        def _():
            remote(mbuf.at[:, :, pl.ds(0, BX)], mm.at[u], ms.at[0, u], mr.at[0, u], u, t).wait_recv()
            remote(sq.at[u], mq.at[u], ms.at[1, u], mr.at[1, u], u, t).wait_recv()

        for p in range(9):
            if p < 8:
                a, b = mm[u, 2 * p].astype(F32), mm[u, 2 * p + 1].astype(F32)
            else:
                a, b = mq[u, 0].astype(F32), mq[u, 1].astype(F32)
            sd[u, p] = jnp.concatenate([a[0:8], b[0:8]], axis=0).astype(BF16)
            su[u, p] = jnp.concatenate([a[24:32], b[24:32]], axis=0).astype(BF16)
        for ok_to, _, copy in relay_copies(u):
            pl.when(ok_to)(copy.start)

    ext_lane = lanes((48, BX))

    @pl.when(jnp.logical_not(has_up))
    def _():
        mu[...] = jnp.zeros(mu.shape, BF16)

    @pl.when(jnp.logical_not(has_down))
    def _():
        md[...] = jnp.zeros(md.shape, BF16)

    def ratio(values, blurred):
        return jnp.where(values > 0, values / blurred, 0.0).astype(BF16)

    def assemble(u):
        cu, cd = mu[u, 8].astype(F32), md[u, 8].astype(F32)
        for q in range(2):
            rows8 = slice(8 * q, 8 * q + 8)
            edge = jnp.concatenate([cu[rows8], mq[u, q].astype(F32), cd[rows8]], axis=0)
            for k in range(8):
                z = 8 * q + k
                side = pltpu.roll(edge, BX - 16 * k, 1) if k else edge
                side = jnp.where((ext_lane < 8) | (ext_lane >= 120), side, 0.0)
                mext[u, z, :, BX:] = side.astype(BF16)
                rt[z, :, BX:] = ratio(side, bl[u, z, :, BX:])
                r = slice(8 * (z % 2), 8 * (z % 2) + 8)
                main = jnp.concatenate(
                    [mu[u, z // 2].astype(F32)[r], mm[u, z].astype(F32), md[u, z // 2].astype(F32)[r]], axis=0
                )
                mext[u, z, :, :BX] = main.astype(BF16)
                rt[z, :, :BX] = ratio(main, bl[u, z, :, :BX])

    def correct(u, ratios):
        weight = pb[u, 8:9, :]
        rows = jnp.dot(ratios.reshape(768, 256), xb[u], preferred_element_type=F32).astype(BF16)
        rows = rows.reshape(NZ, 48, BX)
        chunks = jnp.concatenate([rows[:, 0:32].reshape(512, BX), rows[:, 16:48].reshape(512, BX)], axis=1)
        back = jnp.dot(wb[u], chunks, preferred_element_type=F32)
        for c in range(2):
            log_back = weight * jnp.log(back[:, BX * c : BX * c + BX])
            acc[:, 16 * c : 16 * c + 16, :] += log_back.reshape(NZ, 16, BX)

    count = pb[0, 8:9, :]
    for u in range(1, NV):
        count = count + pb[u, 8:9, :]

    get_own.wait()
    receive_field(0)
    acc[...] = jnp.zeros(acc.shape, F32)

    def source_view(s):
        return lax.rem(v + NV - s, NV)

    def first_forward(s, carry):
        u = source_view(s)
        full = blur(0, u)
        for c in range(3):
            bl[u, :, 16 * c : 16 * c + 16, :] = full[256 * c : 256 * c + 256].reshape(NZ, 16, 256)
        pl.when(s >= 4)(lambda: relay(source_view(s - 4)))
        return carry

    lax.fori_loop(0, NV, first_forward, 0)

    def first_backward(s, carry):
        u = source_view(s)
        pl.when(s < 4)(lambda: relay(source_view(s + 4)))
        for _, ok_from, copy in relay_copies(u):
            pl.when(ok_from)(copy.wait_recv)
        assemble(u)
        correct(u, rt[...])
        return carry

    lax.fori_loop(0, NV, first_backward, 0)
    for z in range(NZ):
        cur[z] = est[z] * jnp.exp(acc[z] / count)
    pack_field(1, cur)
    send_field(1)
    receive_field(1)
    acc[...] = jnp.zeros(acc.shape, F32)

    def second(u, carry):
        full = blur(1, u)
        for c in range(3):
            part = full[256 * c : 256 * c + 256].reshape(NZ, 16, 256)
            rt[:, 16 * c : 16 * c + 16, :] = ratio(mext[u, :, 16 * c : 16 * c + 16, :].astype(F32), part)
        correct(u, rt[...])
        return carry

    lax.fori_loop(0, NV, second, 0)
    for z in range(NZ):
        out[z] = cur[z] * jnp.exp(acc[z] / count)

    for it in range(ITERS):
        for ok_to, _, _, copy in field_copies(it):
            pl.when(ok_to)(copy.wait_send)

    def drain(s, carry):
        d = lax.rem(v + s, NV)

        @pl.when(d != v)
        def _():
            remote(pb.at[v], pb.at[v], ps.at[d], pr.at[d], d, t).wait_send()
            remote(mbuf.at[:, :, pl.ds(0, BX)], mm.at[v], ms.at[0, d], mr.at[0, d], d, t).wait_send()
            remote(sq.at[d], mq.at[v], ms.at[1, d], mr.at[1, d], d, t).wait_send()

        for ok_to, _, copy in relay_copies(d):
            pl.when(ok_to)(copy.wait_send)
        return carry

    lax.fori_loop(0, NV, drain, 0)


def body(estimate, measured, psf_z, psf_xy, offsets, coverage):
    scratch = [
        ((NZ, TY, NV * BX), BF16), ((NV, 16, BX), F32),
        ((2, NZ, 64, 256), BF16), ((2, 2, 64, BX), BF16), ((2, 2, 64, BX), BF16),
        ((2, 2, TY, BX), BF16), ((2, 2, TY, BX), BF16),
        ((NV, NZ, TY, BX), BF16), ((NV, 2, TY, BX), BF16), ((NV, 9, 16, BX), BF16), ((NV, 9, 16, BX), BF16),
        ((NV, 2, TY, BX), BF16), ((NV, 9, 16, BX), BF16), ((NV, 9, 16, BX), BF16),
        ((2, 128, BX), F32), ((2, 128, BX), F32), ((2, 128, 512), F32), ((2, 128, 512), F32),
        ((NV, 256, 512), BF16), ((NV, 256, 512), BF16), ((NV, 256, 256), BF16), ((NV, 256, BX), BF16),
        ((NV, NZ, 48, 256), F32), ((NV, NZ, 48, 256), BF16), ((NZ, 48, 256), BF16), ((NZ, TY, BX), F32), ((NZ, TY, BX), F32),
    ]
    dma = pltpu.SemaphoreType.DMA
    return pl.pallas_call(
        kernel,
        out_shape=jax.ShapeDtypeStruct(estimate.shape, F32),
        in_specs=[pl.BlockSpec(memory_space=pl.ANY)] * 6,
        out_specs=pl.BlockSpec(memory_space=pltpu.VMEM),
        scratch_shapes=[
            pltpu.VMEM((NZ, TY, BX), F32),
            pltpu.SMEM((1, KZ), F32),
            pltpu.SMEM((1, 2, KXY), F32),
            pltpu.SMEM((1, 2), jnp.int32),
            pltpu.SMEM((1, 1), jnp.int32),
        ]
        + [pltpu.VMEM(s, d) for s, d in scratch]
        + [dma((7,)), dma((NV,)), dma((NV,)), dma((2, 8)), dma((2, 8)), dma((4, NV)), dma((4, NV))],
        compiler_params=pltpu.CompilerParams(
            collective_id=0, has_side_effects=True, vmem_limit_bytes=48 * 1024 * 1024
        ),
    )(estimate, measured, psf_z, psf_xy, offsets, coverage)


def solution(mesh):
    placed = (
        P(None, "tile", "view"),
        P("view", None, "tile", None),
        P("view", None),
        P("view", None, None),
        P("view", None),
        P("view", "tile"),
    )
    return jax.shard_map(
        body, mesh=mesh, in_specs=placed, out_specs=P(None, "tile", "view"), check_vma=False
    )
```

time: 66.8 us -> 56.7 us (0.85)
  Pallas kernels: 62.2 us -> 52 us
    pallas_call x1, Pallas kernels: 62.2 us -> 52 us  [body(): pl.pallas_call(kernel, out_shape=jax.ShapeDtypeStruct(estimate.shape, F32...]
where the time goes in v2:
time: 56.7 us; the launch traced here: 56.2 us
  Pallas kernels  52 us (92%)
  local copies, waits for them, and re-layouts  3.53 us (6%)
  between operations  0.72 us (1%)
    pallas_call x1, Pallas kernels, body(): pl.pallas_call(kernel, out_shape=jax.ShapeDtypeStruct(estimate.shape, F32...  52 us
    unnamed x11, local copies, waits for them, and re-layouts  3.53 us

profile of v2, /device:TPU:48, one launch (start us, length us, event | category | flops | bytes accessed | tf_op | source)
XLA Modules:
  0.0 56.2 jit_solution(17480029263564939536)
XLA Ops:
  0.0 0.0 copy-start.2
  0.0 0.0 copy-start.3
  0.7 0.0 copy-done.2
  0.7 0.0 copy-done.3
  0.7 0.0 copy-start
  0.7 1.2 %copy-done = bf16[1,16,32,1024]{3,2,1,0:T(8,128)(2,1)S(1)} copy-done((bf16[1,16,32,1024]{3,2,1,0:T(8,128)(2,1)S(1)}, bf16[1,16,32,1024]{3,2,1,0:T(8,128)(2,1)}, u32[]{:S(2)}) %copy-start) | copy-done | bytes 1048600
  1.9 0.0 copy-start.1
  1.9 0.9 %copy-done.1 = f32[16,32,128]{2,1,0:T(8,128)S(1)} copy-done((f32[16,32,128]{2,1,0:T(8,128)S(1)}, f32[16,32,128]{2,1,0:T(8,128)}, u32[]{:S(2)}) %copy-start.1) | copy-done | bytes 262168
  2.9 0.0 copy-start.4
  2.9 0.7 %copy-done.4 = s32[1,2]{1,0:T(1,128)S(1)} copy-done((s32[1,2]{1,0:T(1,128)S(1)}, s32[1,2]{1,0:T(1,128)}, u32[]{:S(2)}) %copy-start.4) | copy-done | bytes 32
  3.5 52.0 %shard_map.64 = f32[16,32,128]{2,1,0:T(8,128)S(1)} custom-call(f32[16,32,128]{2,1,0:T(8,128)S(1)} %copy-done.1, bf16[1,16,32,1024]{3,2,1,0:T(8,128)(2,1)S(1)} %copy-done, f32[1,65]{1,0:T(1,128)S(1)} %copy-done.3, f32[1,2,9]{2,1,0:T(2,128)S(1)} %copy-done.2, s32[1,2]{1,0:T(1,128)S(1)} %copy-done.4, s32[1,1]{1,0:T(1,128)S(6)} %copy.8.cov_hbm), custom_call_target="tpu_custom_call" | custom-call | tf_op jit(solution)/shard_map/pallas_call | solution.py:389
  55.5 0.7 %copy.9 = f32[16,32,128]{2,1,0:T(8,128)} copy(f32[16,32,128]{2,1,0:T(8,128)S(1)} %shard_map.64) | data formatting | bytes 524288
Async XLA Ops:
  0.0 0.7 %copy-start.2 = (f32[1,2,9]{2,1,0:T(2,128)S(1)}, f32[1,2,9]{2,1,0:T(2,128)}, u32[]{:S(2)}) copy-start(f32[1,2,9]{2,1,0:T(2,128)} %pxy_hbm.1) | copy-start | bytes 220
  0.0 0.7 %copy-start.3 = (f32[1,65]{1,0:T(1,128)S(1)}, f32[1,65]{1,0:T(1,128)}, u32[]{:S(2)}) copy-start(f32[1,65]{1,0:T(1,128)} %pz_hbm.1) | copy-start | bytes 784
  0.7 1.2 %copy-start = (bf16[1,16,32,1024]{3,2,1,0:T(8,128)(2,1)S(1)}, bf16[1,16,32,1024]{3,2,1,0:T(8,128)(2,1)}, u32[]{:S(2)}) copy-start(bf16[1,16,32,1024]{3,2,1,0:T(8,128)(2,1)} %meas.1) | copy-start | bytes 3145732
  1.9 0.9 %copy-start.1 = (f32[16,32,128]{2,1,0:T(8,128)S(1)}, f32[16,32,128]{2,1,0:T(8,128)}, u32[]{:S(2)}) copy-start(f32[16,32,128]{2,1,0:T(8,128)} %est_hbm.1) | copy-start | bytes 786436
  2.9 0.7 %copy-start.4 = (s32[1,2]{1,0:T(1,128)S(1)}, s32[1,2]{1,0:T(1,128)}, u32[]{:S(2)}) copy-start(s32[1,2]{1,0:T(1,128)} %offs_hbm.1) | copy-start | bytes 28

commit v3 on v2

--- a/solution.py
+++ b/solution.py
@@ -44,6 +44,14 @@
         return pltpu.make_async_remote_copy(
             src_ref=src, dst_ref=dst, send_sem=send, recv_sem=recv, device_id=(dv, dt), device_id_type=MESH
         )
+
+    half, spot = v // 4, lax.rem(v, 4)
+
+    def target_view(s):
+        return lax.rem(half + s // 4, 2) * 4 + lax.rem(spot + s, 4)
+
+    def source_view(s):
+        return lax.rem(half + s // 4, 2) * 4 + lax.rem(spot + 8 - s, 4)
 
     own_cols = pl.ds(pl.multiple_of(v * BX, BX), BX)
     get_all = pltpu.make_async_copy(meas.at[0], mbuf, loc.at[0])
@@ -165,7 +173,18 @@
     pack_field(0, est)
     get_all.wait()
 
-    def pack_columns(d, carry):
+    pl.semaphore_wait(barrier, len(partners))
+    for s in range(1, NV):
+        d = target_view(s)
+        remote(pb.at[v], pb.at[v], ps.at[d], pr.at[v], d, t).start()
+    send_field(0)
+    for s in range(1, NV):
+        d = target_view(s)
+        cols = pl.ds(pl.multiple_of(d * BX, BX), BX)
+        remote(mbuf.at[:, :, cols], mm.at[v], ms.at[0, d], mr.at[0, v], d, t).start()
+
+    def pack_columns(s, carry):
+        d = target_view(s)
         after = pl.ds(pl.multiple_of(jnp.minimum(d + 1, NV - 1) * BX, BX), BX)
         before = pl.ds(pl.multiple_of(jnp.maximum(d - 1, 0) * BX, BX), BX)
         take_after = (plane_lane < 8) & (d < NV - 1)
@@ -180,21 +199,15 @@
                 )
                 packed = packed + (pltpu.roll(edge, 16 * k, 1) if k else edge)
             sq[d, q] = packed.astype(BF16)
+
+        @pl.when(s > 0)
+        def _():
+            remote(sq.at[d], mq.at[v], ms.at[1, d], mr.at[1, v], d, t).start()
+
         return carry
 
     lax.fori_loop(0, NV, pack_columns, 0)
     mq[v] = sq[v]
-
-    pl.semaphore_wait(barrier, len(partners))
-    for s in range(1, NV):
-        d = lax.rem(v + s, NV)
-        remote(pb.at[v], pb.at[v], ps.at[d], pr.at[v], d, t).start()
-    send_field(0)
-    for s in range(1, NV):
-        d = lax.rem(v + s, NV)
-        cols = pl.ds(pl.multiple_of(d * BX, BX), BX)
-        remote(mbuf.at[:, :, cols], mm.at[v], ms.at[0, d], mr.at[0, v], d, t).start()
-        remote(sq.at[d], mq.at[v], ms.at[1, d], mr.at[1, v], d, t).start()
 
     for s in range(1, NV):
         u = lax.rem(v + s, NV)
@@ -309,32 +322,35 @@
         count = count + pb[u, 8:9, :]
 
     get_own.wait()
+
+    def relay_step(s, carry):
+        relay(source_view(s))
+        return carry
+
+    lax.fori_loop(0, 4, relay_step, 0)
     receive_field(0)
     acc[...] = jnp.zeros(acc.shape, F32)
-
-    def source_view(s):
-        return lax.rem(v + NV - s, NV)
 
     def first_forward(s, carry):
         u = source_view(s)
         full = blur(0, u)
         for c in range(3):
             bl[u, :, 16 * c : 16 * c + 16, :] = full[256 * c : 256 * c + 256].reshape(NZ, 16, 256)
-        pl.when(s >= 4)(lambda: relay(source_view(s - 4)))
         return carry
 
     lax.fori_loop(0, NV, first_forward, 0)
 
     def first_backward(s, carry):
         u = source_view(s)
-        pl.when(s < 4)(lambda: relay(source_view(s + 4)))
         for _, ok_from, copy in relay_copies(u):
             pl.when(ok_from)(copy.wait_recv)
         assemble(u)
         correct(u, rt[...])
         return carry
 
-    lax.fori_loop(0, NV, first_backward, 0)
+    lax.fori_loop(0, 4, first_backward, 0)
+    lax.fori_loop(4, NV, relay_step, 0)
+    lax.fori_loop(4, NV, first_backward, 0)
     for z in range(NZ):
         cur[z] = est[z] * jnp.exp(acc[z] / count)
     pack_field(1, cur)
@@ -350,7 +366,7 @@
         correct(u, rt[...])
         return carry
 
-    lax.fori_loop(0, NV, second, 0)
+    lax.fori_loop(0, NV, second, 0, unroll=8)
     for z in range(NZ):
         out[z] = cur[z] * jnp.exp(acc[z] / count)
 
@@ -401,7 +417,7 @@
         + [pltpu.VMEM(s, d) for s, d in scratch]
         + [dma((7,)), dma((NV,)), dma((NV,)), dma((2, 8)), dma((2, 8)), dma((4, NV)), dma((4, NV))],
         compiler_params=pltpu.CompilerParams(
-            collective_id=0, has_side_effects=True, vmem_limit_bytes=48 * 1024 * 1024
+            collective_id=0, has_side_effects=True, vmem_limit_bytes=60 * 1024 * 1024
         ),
     )(estimate, measured, psf_z, psf_xy, offsets, coverage)
 

time: 56.7 us -> 54.7 us (0.965)
  local copies, waits for them, and re-layouts: 3.53 us -> 1.67 us
    unnamed x11 -> x1, local copies, waits for them, and re-layouts: 3.53 us -> 1.67 us
where the time goes in v3:
time: 54.7 us; the launch traced here: 54.5 us
  Pallas kernels  52.1 us (95%)
  local copies, waits for them, and re-layouts  1.67 us (3%)
  between operations  0.66 us (1%)
    pallas_call x1, Pallas kernels, body(): pl.pallas_call(kernel, out_shape=jax.ShapeDtypeStruct(estimate.shape, F32...  52.1 us
    unnamed x1, local copies, waits for them, and re-layouts  1.67 us

profile of v3, /device:TPU:48, one launch (start us, length us, event | category | flops | bytes accessed | tf_op | source)
XLA Modules:
  0.0 54.5 jit_solution(5065169271683945674)
XLA Ops:
  0.7 52.1 %shard_map.64 = f32[16,32,128]{2,1,0:T(8,128)} custom-call(f32[16,32,128]{2,1,0:T(8,128)} %est_hbm.1, bf16[1,16,32,1024]{3,2,1,0:T(8,128)(2,1)} %meas.1, f32[1,65]{1,0:T(1,128)} %pz_hbm.1, f32[1,2,9]{2,1,0:T(2,128)} %pxy_hbm.1, s32[1,2]{1,0:T(1,128)} %offs_hbm.1, s32[1,1]{1,0:T(1,128)S(6)} %copy.8.cov_hbm), custom_call_target="tpu_custom_call" | custom-call | tf_op jit(solution)/shard_map/pallas_call | solution.py:405
  52.8 1.7 %copy.9 = f32[16,32,128]{2,1,0:T(8,128)} copy(f32[16,32,128]{2,1,0:T(8,128)} %shard_map.64) | data formatting | bytes 524288

commit v4 on v3

--- a/solution.py
+++ b/solution.py
@@ -32,9 +32,9 @@
 def kernel(
     est_hbm, meas, pz_hbm, pxy_hbm, offs_hbm, cov_hbm, out,
     est, pz, pxy, offs, cov,
-    mbuf, pb, fld, hr, hl, sr, sl, mm, mq, mu, md, sq, su, sd,
+    mbuf, pb, fld, hr, hl, sr, sl, mm, mq, mu, md, sq, su, sd, sx,
     rz, ry, az, ay, wf, wb, xf, xb, bl, mext, rt, acc, cur,
-    loc, ps, pr, fs, fr, ms, mr,
+    loc, ps, pr, fs, fr, ms, mr, mx,
 ):
     v, t = lax.axis_index("view"), lax.axis_index("tile")
     has_up, has_down = t > 0, t < NT - 1
@@ -52,6 +52,11 @@
 
     def source_view(s):
         return lax.rem(half + s // 4, 2) * 4 + lax.rem(spot + 8 - s, 4)
+
+    odd = lax.rem(t, 2) == 1
+    cross = lax.rem(t + NT - 1 + 2 * lax.rem(t, 2), NT)
+    straight_down = odd & (half == 1) & has_down
+    straight_up = jnp.logical_not(odd) & (half == 0) & has_up
 
     own_cols = pl.ds(pl.multiple_of(v * BX, BX), BX)
     get_all = pltpu.make_async_copy(meas.at[0], mbuf, loc.at[0])
@@ -71,6 +76,7 @@
     up_tile, down_tile = lax.rem(t + NT - 1, NT), lax.rem(t + 1, NT)
     partners = [(lax.rem(v + s, NV), t) for s in range(1, NV)]
     partners += [(lax.rem(v + s, NV), dt) for s in (0, 1, NV - 1) for dt in (up_tile, down_tile)]
+    partners += [(lax.rem(half + 1, 2) * 4 + k, cross) for k in range(4)]
     for partner in partners:
         pl.semaphore_signal(barrier, inc=1, device_id=partner, device_id_type=MESH)
     for copy in small[:4]:
@@ -135,6 +141,8 @@
     def pack_field(it, source):
         for z in range(NZ):
             fld[it, z, 16:48, 0:BX] = source[z].astype(BF16)
+
+    def pack_sides(it, source):
         for q in range(2):
             head = jnp.zeros((TY, BX), F32)
             tail = jnp.zeros((TY, BX), F32)
@@ -147,18 +155,22 @@
             sr[it, q] = head.astype(BF16)
             sl[it, q] = tail.astype(BF16)
 
-    def send_field(it):
-        for ok_to, _, _, copy in field_copies(it):
+    def send_field(it, which):
+        for ok_to, _, _, copy in field_copies(it)[which]:
             pl.when(ok_to)(copy.start)
 
-    def receive_field(it):
-        for _, ok_from, dst, copy in field_copies(it):
+    rows, sides = slice(0, 2), slice(2, 8)
+
+    def arrived(it, which):
+        for _, ok_from, dst, copy in field_copies(it)[which]:
             pl.when(ok_from)(copy.wait_recv)
 
             @pl.when(jnp.logical_not(ok_from))
             def _():
                 dst[...] = jnp.zeros(dst.shape, BF16)
 
+    def receive_field(it):
+        arrived(it, sides)
         for q in range(2):
             right = hr[it, q].astype(F32)
             left = hl[it, q].astype(F32)
@@ -168,20 +180,28 @@
                     both = pltpu.roll(both, BX - 16 * k, 1)
                 both = jnp.where((wide_lane < 16) | (wide_lane >= 112), both, 0.0)
                 fld[it, 8 * q + k, :, BX:] = both.astype(BF16)
+        arrived(it, rows)
 
     small[4].wait()
     pack_field(0, est)
+    pack_sides(0, est)
     get_all.wait()
 
     pl.semaphore_wait(barrier, len(partners))
     for s in range(1, NV):
         d = target_view(s)
         remote(pb.at[v], pb.at[v], ps.at[d], pr.at[v], d, t).start()
-    send_field(0)
+    send_field(0, slice(0, 8))
     for s in range(1, NV):
         d = target_view(s)
         cols = pl.ds(pl.multiple_of(d * BX, BX), BX)
         remote(mbuf.at[:, :, cols], mm.at[v], ms.at[0, d], mr.at[0, v], d, t).start()
+
+    def straight_copies(d):
+        return (
+            (straight_down, remote(sx.at[d], mu.at[v], mx.at[d], mr.at[2, v], d, t + 1)),
+            (straight_up, remote(sx.at[d], md.at[v], mx.at[d], mr.at[3, v], d, t - 1)),
+        )
 
     def pack_columns(s, carry):
         d = target_view(s)
@@ -189,6 +209,7 @@
         before = pl.ds(pl.multiple_of(jnp.maximum(d - 1, 0) * BX, BX), BX)
         take_after = (plane_lane < 8) & (d < NV - 1)
         take_before = (plane_lane >= 120) & (d > 0)
+        corner = []
         for q in range(2):
             packed = jnp.zeros((TY, BX), F32)
             for k in range(8):
@@ -198,11 +219,28 @@
                     jnp.where(take_before, mbuf[z, :, before].astype(F32), 0.0),
                 )
                 packed = packed + (pltpu.roll(edge, 16 * k, 1) if k else edge)
+            corner.append(packed)
             sq[d, q] = packed.astype(BF16)
 
         @pl.when(s > 0)
         def _():
             remote(sq.at[d], mq.at[v], ms.at[1, d], mr.at[1, v], d, t).start()
+
+        @pl.when((s >= 4) & (straight_up | straight_down))
+        def _():
+            here = pl.ds(pl.multiple_of(d * BX, BX), BX)
+
+            def edge_rows(a):
+                return jnp.where(odd, a[24:32], a[0:8])
+
+            for p in range(9):
+                if p < 8:
+                    a, b = mbuf[2 * p, :, here].astype(F32), mbuf[2 * p + 1, :, here].astype(F32)
+                else:
+                    a, b = corner
+                sx[d, p] = jnp.concatenate([edge_rows(a), edge_rows(b)], axis=0).astype(BF16)
+            for ok_to, copy in straight_copies(d):
+                pl.when(ok_to)(copy.start)
 
         return carry
 
@@ -232,9 +270,9 @@
     n = lanes((BX, 512))
     spread_z = (m == n // 32 + 32).astype(F32)
     spread_y = (m == n % 32).astype(F32)
-    for half in range(2):
-        az[half] = jnp.dot(rz[half], spread_z, precision=EXACT, preferred_element_type=F32)
-        ay[half] = jnp.dot(ry[half], spread_y, precision=EXACT, preferred_element_type=F32)
+    for way in range(2):
+        az[way] = jnp.dot(rz[way], spread_z, precision=EXACT, preferred_element_type=F32)
+        ay[way] = jnp.dot(ry[way], spread_y, precision=EXACT, preferred_element_type=F32)
 
     def depth_rows(u, carry):
         z16 = pl.ds(pl.multiple_of(u * 16, 16), 16)
@@ -255,9 +293,12 @@
         return jnp.dot(jnp.concatenate(parts, axis=0), xf[u], preferred_element_type=F32)
 
     def relay_copies(u):
+        far = u // 4 != half
+        skip_down = far & odd & (half == 0)
+        skip_up = far & jnp.logical_not(odd) & (half == 1)
         return (
-            (has_down, has_up, remote(su.at[u], mu.at[u], ms.at[2, u], mr.at[2, u], v, t + 1)),
-            (has_up, has_down, remote(sd.at[u], md.at[u], ms.at[3, u], mr.at[3, u], v, t - 1)),
+            (has_down & jnp.logical_not(skip_down), has_up, remote(su.at[u], mu.at[u], ms.at[2, u], mr.at[2, u], v, t + 1)),
+            (has_up & jnp.logical_not(skip_up), has_down, remote(sd.at[u], md.at[u], ms.at[3, u], mr.at[3, u], v, t - 1)),
         )
 
     def relay(u):
@@ -354,9 +395,29 @@
     for z in range(NZ):
         cur[z] = est[z] * jnp.exp(acc[z] / count)
     pack_field(1, cur)
-    send_field(1)
+    send_field(1, rows)
+    pack_sides(1, cur)
+    send_field(1, sides)
+    acc[...] = jnp.zeros(acc.shape, F32)
+
+    def drain(s, carry):
+        d = lax.rem(v + s, NV)
+
+        @pl.when(d != v)
+        def _():
+            remote(pb.at[v], pb.at[v], ps.at[d], pr.at[d], d, t).wait_send()
+            remote(mbuf.at[:, :, pl.ds(0, BX)], mm.at[v], ms.at[0, d], mr.at[0, d], d, t).wait_send()
+            remote(sq.at[d], mq.at[v], ms.at[1, d], mr.at[1, d], d, t).wait_send()
+
+        for ok_to, _, copy in relay_copies(d):
+            pl.when(ok_to)(copy.wait_send)
+        for ok_to, copy in straight_copies(d):
+            pl.when(ok_to & (d // 4 != half))(copy.wait_send)
+        return carry
+
+    lax.fori_loop(0, NV, drain, 0)
+
     receive_field(1)
-    acc[...] = jnp.zeros(acc.shape, F32)
 
     def second(u, carry):
         full = blur(1, u)
@@ -374,21 +435,6 @@
         for ok_to, _, _, copy in field_copies(it):
             pl.when(ok_to)(copy.wait_send)
 
-    def drain(s, carry):
-        d = lax.rem(v + s, NV)
-
-        @pl.when(d != v)
-        def _():
-            remote(pb.at[v], pb.at[v], ps.at[d], pr.at[d], d, t).wait_send()
-            remote(mbuf.at[:, :, pl.ds(0, BX)], mm.at[v], ms.at[0, d], mr.at[0, d], d, t).wait_send()
-            remote(sq.at[d], mq.at[v], ms.at[1, d], mr.at[1, d], d, t).wait_send()
-
-        for ok_to, _, copy in relay_copies(d):
-            pl.when(ok_to)(copy.wait_send)
-        return carry
-
-    lax.fori_loop(0, NV, drain, 0)
-
 
 def body(estimate, measured, psf_z, psf_xy, offsets, coverage):
     scratch = [
@@ -396,7 +442,7 @@
         ((2, NZ, 64, 256), BF16), ((2, 2, 64, BX), BF16), ((2, 2, 64, BX), BF16),
         ((2, 2, TY, BX), BF16), ((2, 2, TY, BX), BF16),
         ((NV, NZ, TY, BX), BF16), ((NV, 2, TY, BX), BF16), ((NV, 9, 16, BX), BF16), ((NV, 9, 16, BX), BF16),
-        ((NV, 2, TY, BX), BF16), ((NV, 9, 16, BX), BF16), ((NV, 9, 16, BX), BF16),
+        ((NV, 2, TY, BX), BF16), ((NV, 9, 16, BX), BF16), ((NV, 9, 16, BX), BF16), ((NV, 9, 16, BX), BF16),
         ((2, 128, BX), F32), ((2, 128, BX), F32), ((2, 128, 512), F32), ((2, 128, 512), F32),
         ((NV, 256, 512), BF16), ((NV, 256, 512), BF16), ((NV, 256, 256), BF16), ((NV, 256, BX), BF16),
         ((NV, NZ, 48, 256), F32), ((NV, NZ, 48, 256), BF16), ((NZ, 48, 256), BF16), ((NZ, TY, BX), F32), ((NZ, TY, BX), F32),
@@ -415,7 +461,7 @@
             pltpu.SMEM((1, 1), jnp.int32),
         ]
         + [pltpu.VMEM(s, d) for s, d in scratch]
-        + [dma((7,)), dma((NV,)), dma((NV,)), dma((2, 8)), dma((2, 8)), dma((4, NV)), dma((4, NV))],
+        + [dma((7,)), dma((NV,)), dma((NV,)), dma((2, 8)), dma((2, 8)), dma((4, NV)), dma((4, NV)), dma((NV,))],
         compiler_params=pltpu.CompilerParams(
             collective_id=0, has_side_effects=True, vmem_limit_bytes=60 * 1024 * 1024
         ),

time: 54.7 us -> 53.4 us (0.976)
  Pallas kernels: 52.1 us -> 50.7 us
    pallas_call x1, Pallas kernels: 52.1 us -> 50.7 us  [body(): pl.pallas_call(kernel, out_shape=jax.ShapeDtypeStruct(estimate.shape, F32...]
where the time goes in v4:
time: 53.4 us; the launch traced here: 53 us
  Pallas kernels  50.7 us (95%)
  local copies, waits for them, and re-layouts  1.67 us (3%)
  between operations  0.66 us (1%)
    pallas_call x1, Pallas kernels, body(): pl.pallas_call(kernel, out_shape=jax.ShapeDtypeStruct(estimate.shape, F32...  50.7 us
    unnamed x1, local copies, waits for them, and re-layouts  1.67 us

profile of v4, /device:TPU:48, one launch (start us, length us, event | category | flops | bytes accessed | tf_op | source)
XLA Modules:
  0.0 53.0 jit_solution(1227593365241875578)
XLA Ops:
  0.7 50.7 %shard_map.64 = f32[16,32,128]{2,1,0:T(8,128)} custom-call(f32[16,32,128]{2,1,0:T(8,128)} %est_hbm.1, bf16[1,16,32,1024]{3,2,1,0:T(8,128)(2,1)} %meas.1, f32[1,65]{1,0:T(1,128)} %pz_hbm.1, f32[1,2,9]{2,1,0:T(2,128)} %pxy_hbm.1, s32[1,2]{1,0:T(1,128)} %offs_hbm.1, s32[1,1]{1,0:T(1,128)S(6)} %copy.8.cov_hbm), custom_call_target="tpu_custom_call" | custom-call | tf_op jit(solution)/shard_map/pallas_call | solution.py:451
  51.4 1.7 %copy.9 = f32[16,32,128]{2,1,0:T(8,128)} copy(f32[16,32,128]{2,1,0:T(8,128)} %shard_map.64) | data formatting | bytes 524288

commit v5 on v4

--- a/solution.py
+++ b/solution.py
@@ -379,7 +379,7 @@
             bl[u, :, 16 * c : 16 * c + 16, :] = full[256 * c : 256 * c + 256].reshape(NZ, 16, 256)
         return carry
 
-    lax.fori_loop(0, NV, first_forward, 0)
+    lax.fori_loop(0, NV, first_forward, 0, unroll=8)
 
     def first_backward(s, carry):
         u = source_view(s)
@@ -389,9 +389,8 @@
         correct(u, rt[...])
         return carry
 
-    lax.fori_loop(0, 4, first_backward, 0)
     lax.fori_loop(4, NV, relay_step, 0)
-    lax.fori_loop(4, NV, first_backward, 0)
+    lax.fori_loop(0, NV, first_backward, 0, unroll=4)
     for z in range(NZ):
         cur[z] = est[z] * jnp.exp(acc[z] / count)
     pack_field(1, cur)

time: 53.4 us -> 50.1 us (0.938)
  Pallas kernels: 50.7 us -> 47.6 us
    pallas_call x1, Pallas kernels: 50.7 us -> 47.6 us  [body(): pl.pallas_call(kernel, out_shape=jax.ShapeDtypeStruct(estimate.shape, F32...]
where the time goes in v5:
time: 50.1 us; the launch traced here: 50 us
  Pallas kernels  47.6 us (95%)
  local copies, waits for them, and re-layouts  1.67 us (3%)
  between operations  0.66 us (1%)
    pallas_call x1, Pallas kernels, body(): pl.pallas_call(kernel, out_shape=jax.ShapeDtypeStruct(estimate.shape, F32...  47.6 us
    unnamed x1, local copies, waits for them, and re-layouts  1.67 us

profile of v5, /device:TPU:48, one launch (start us, length us, event | category | flops | bytes accessed | tf_op | source)
XLA Modules:
  0.0 50.0 jit_solution(14032141121829132664)
XLA Ops:
  0.7 47.6 %shard_map.64 = f32[16,32,128]{2,1,0:T(8,128)} custom-call(f32[16,32,128]{2,1,0:T(8,128)} %est_hbm.1, bf16[1,16,32,1024]{3,2,1,0:T(8,128)(2,1)} %meas.1, f32[1,65]{1,0:T(1,128)} %pz_hbm.1, f32[1,2,9]{2,1,0:T(2,128)} %pxy_hbm.1, s32[1,2]{1,0:T(1,128)} %offs_hbm.1, s32[1,1]{1,0:T(1,128)S(6)} %copy.8.cov_hbm), custom_call_target="tpu_custom_call" | custom-call | tf_op jit(solution)/shard_map/pallas_call | solution.py:450
  48.3 1.7 %copy.9 = f32[16,32,128]{2,1,0:T(8,128)} copy(f32[16,32,128]{2,1,0:T(8,128)} %shard_map.64) | data formatting | bytes 524288

commit v6 on v5

--- a/solution.py
+++ b/solution.py
@@ -55,8 +55,8 @@
 
     odd = lax.rem(t, 2) == 1
     cross = lax.rem(t + NT - 1 + 2 * lax.rem(t, 2), NT)
-    straight_down = odd & (half == 1) & has_down
-    straight_up = jnp.logical_not(odd) & (half == 0) & has_up
+    straight_down = t < 0
+    straight_up = t < 0
 
     own_cols = pl.ds(pl.multiple_of(v * BX, BX), BX)
     get_all = pltpu.make_async_copy(meas.at[0], mbuf, loc.at[0])
@@ -76,7 +76,6 @@
     up_tile, down_tile = lax.rem(t + NT - 1, NT), lax.rem(t + 1, NT)
     partners = [(lax.rem(v + s, NV), t) for s in range(1, NV)]
     partners += [(lax.rem(v + s, NV), dt) for s in (0, 1, NV - 1) for dt in (up_tile, down_tile)]
-    partners += [(lax.rem(half + 1, 2) * 4 + k, cross) for k in range(4)]
     for partner in partners:
         pl.semaphore_signal(barrier, inc=1, device_id=partner, device_id_type=MESH)
     for copy in small[:4]:
@@ -294,8 +293,8 @@
 
     def relay_copies(u):
         far = u // 4 != half
-        skip_down = far & odd & (half == 0)
-        skip_up = far & jnp.logical_not(odd) & (half == 1)
+        skip_down = far & (t < 0)
+        skip_up = far & (t < 0)
         return (
             (has_down & jnp.logical_not(skip_down), has_up, remote(su.at[u], mu.at[u], ms.at[2, u], mr.at[2, u], v, t + 1)),
             (has_up & jnp.logical_not(skip_up), has_down, remote(sd.at[u], md.at[u], ms.at[3, u], mr.at[3, u], v, t - 1)),
@@ -368,7 +367,6 @@
         relay(source_view(s))
         return carry
 
-    lax.fori_loop(0, 4, relay_step, 0)
     receive_field(0)
     acc[...] = jnp.zeros(acc.shape, F32)
 
@@ -379,7 +377,9 @@
             bl[u, :, 16 * c : 16 * c + 16, :] = full[256 * c : 256 * c + 256].reshape(NZ, 16, 256)
         return carry
 
-    lax.fori_loop(0, NV, first_forward, 0, unroll=8)
+    lax.fori_loop(0, 4, first_forward, 0, unroll=4)
+    lax.fori_loop(0, 4, relay_step, 0)
+    lax.fori_loop(4, NV, first_forward, 0, unroll=4)
 
     def first_backward(s, carry):
         u = source_view(s)

time: 50.1 us -> 50 us (level)
  no operation moved by 1% of the time
where the time goes in v6:
time: 50 us; the launch traced here: 49.9 us
  Pallas kernels  47.5 us (95%)
  local copies, waits for them, and re-layouts  1.67 us (3%)
  between operations  0.66 us (1%)
    pallas_call x1, Pallas kernels, body(): pl.pallas_call(kernel, out_shape=jax.ShapeDtypeStruct(estimate.shape, F32...  47.5 us
    unnamed x1, local copies, waits for them, and re-layouts  1.67 us

profile of v6, /device:TPU:48, one launch (start us, length us, event | category | flops | bytes accessed | tf_op | source)
XLA Modules:
  0.0 49.9 jit_solution(14456315439995297551)
XLA Ops:
  0.7 47.5 %shard_map.64 = f32[16,32,128]{2,1,0:T(8,128)} custom-call(f32[16,32,128]{2,1,0:T(8,128)} %est_hbm.1, bf16[1,16,32,1024]{3,2,1,0:T(8,128)(2,1)} %meas.1, f32[1,65]{1,0:T(1,128)} %pz_hbm.1, f32[1,2,9]{2,1,0:T(2,128)} %pxy_hbm.1, s32[1,2]{1,0:T(1,128)} %offs_hbm.1, s32[1,1]{1,0:T(1,128)S(6)} %copy.8.cov_hbm), custom_call_target="tpu_custom_call" | custom-call | tf_op jit(solution)/shard_map/pallas_call | solution.py:450
  48.2 1.7 %copy.9 = f32[16,32,128]{2,1,0:T(8,128)} copy(f32[16,32,128]{2,1,0:T(8,128)} %shard_map.64) | data formatting | bytes 524288
